TPU v7x, 32 devices: a whole 2x2x4 slice. The times are simulated.
32 devices in a mesh: fsdp: 16 (over z, x, core), rep: 2 (over y).
Axes of the slice: x: 2, y: 2, z: 4, core: 2. Of those that a mesh axis runs over, the one named last changes fastest.
Arguments:
- pixels: bfloat16 [32768, 768], P(('fsdp', 'rep')), may hold values from -6 to 6
- image_tokens: int32 [32, 4], P(('fsdp', 'rep')), may hold values from 0 to 900, as said below
- patch_class: int32 [32, 4], P(('fsdp', 'rep')), may hold values from 0 to 1, as said below
- resize_coarse: bfloat16 [768, 3072], replicated, may hold values from -0.21875 to 0.21875
- resize_fine: bfloat16 [192, 3072], replicated, may hold values from -0.4375 to 0.4375
- w_base: float32 [3072, 768], P('fsdp'), may hold values from -0.109375 to 0.109375
- w_qkv: float32 [768, 2304], P('fsdp'), may hold values from -0.21875 to 0.21875
- w_proj: float32 [768, 768], P('fsdp'), may hold values from -0.4375 to 0.4375
- w_fc1: float32 [768, 3072], P('fsdp'), may hold values from -0.21875 to 0.21875
- w_fc2: float32 [3072, 768], P('fsdp'), may hold values from -0.109375 to 0.109375
- small_params: float32 [11, 768], P(None, 'fsdp')
- first_base: float32 [3072, 768], P('fsdp'), may hold values from -0.00048828125 to 0.00048828125
- first_qkv: float32 [768, 2304], P('fsdp'), may hold values from -0.00048828125 to 0.00048828125
- first_proj: float32 [768, 768], P('fsdp'), may hold values from -0.00048828125 to 0.00048828125
- first_fc1: float32 [768, 3072], P('fsdp'), may hold values from -0.00048828125 to 0.00048828125
- first_fc2: float32 [3072, 768], P('fsdp'), may hold values from -0.00048828125 to 0.00048828125
- first_small: float32 [11, 768], P(None, 'fsdp'), may hold values from -0.00048828125 to 0.00048828125
- second_base: float32 [3072, 768], P('fsdp'), may hold values from 5.611059e-09 to 2.2232499e-08
- second_qkv: float32 [768, 2304], P('fsdp'), may hold values from 5.611059e-09 to 2.2232499e-08
- second_proj: float32 [768, 768], P('fsdp'), may hold values from 5.611059e-09 to 2.2232499e-08
- second_fc1: float32 [768, 3072], P('fsdp'), may hold values from 5.611059e-09 to 2.2232499e-08
- second_fc2: float32 [3072, 768], P('fsdp'), may hold values from 5.611059e-09 to 2.2232499e-08
- second_small: float32 [11, 768], P(None, 'fsdp'), may hold values from 5.611059e-09 to 2.2232499e-08
- cotangent: bfloat16 [32768, 768], P(('fsdp', 'rep')), may hold values from -6 to 6
Outputs:
- activations: bfloat16 [32768, 768], P(('fsdp', 'rep'))
- pixel_grad: bfloat16 [32768, 768], P(('fsdp', 'rep'))
- grad_norm: float32 [], replicated
- base_new: float32 [3072, 768], P('fsdp')
- qkv_new: float32 [768, 2304], P('fsdp')
- proj_new: float32 [768, 768], P('fsdp')
- fc1_new: float32 [768, 3072], P('fsdp')
- fc2_new: float32 [3072, 768], P('fsdp')
- small_new: float32 [11, 768], P(None, 'fsdp')
- first_base_new: float32 [3072, 768], P('fsdp')
- first_qkv_new: float32 [768, 2304], P('fsdp')
- first_proj_new: float32 [768, 768], P('fsdp')
- first_fc1_new: float32 [768, 3072], P('fsdp')
- first_fc2_new: float32 [3072, 768], P('fsdp')
- first_small_new: float32 [11, 768], P(None, 'fsdp')
- second_base_new: float32 [3072, 768], P('fsdp')
- second_qkv_new: float32 [768, 2304], P('fsdp')
- second_proj_new: float32 [768, 768], P('fsdp')
- second_fc1_new: float32 [768, 3072], P('fsdp')
- second_fc2_new: float32 [3072, 768], P('fsdp')
- second_small_new: float32 [11, 768], P(None, 'fsdp')
Inputs may be any that keep to these rules, and one draw needn't show every extreme that they name: `image_tokens`: each row holds either one image of 900 tokens with class 1 in slot 0 and empty slots after it, or one to 4 images of 225 tokens with class 0 in the first slots and empty slots (0 tokens) after them; every draw has at least one fine image. `patch_class`: 1 only in slot 0 of a row holding a fine image.
All inputs are finite; a program needn't handle non-finite values.
Results may differ from a plain program's by a relative error of at most 0.019.
Values may be sent and summed in bfloat16 or wider, within the bound.
No kernel may reach another device: no remote copies, remote signals or barrier semaphores. Data moves between devices by JAX's collectives and lax.ppermute only.
A program may use at most 256 MiB of HBM per device.

v0:
```python
import math

import jax
import jax.numpy as jnp
from jax import lax
from jax.sharding import PartitionSpec as P

D = 768
HEADS = 12
HEAD_DIM = 64
FF = 3072
PIXC = 768
PIXF = 192
STEP = 10


EPS_NORM = 1e-06
NEG_BIG = -1000000000.0
RATE = 0.05
RATE_SMALL = 0.5
BETA_ONE = 0.9
BETA_TWO = 0.95
ADAM_EPS = 1e-08
DECAY = 0.05
CLIP_NORM = 1.0


def rows_plan(lengths, classes, count):
    ends = jnp.cumsum(lengths)
    positions = jnp.arange(count, dtype=jnp.int32)
    segment = jnp.sum((positions[:, None] >= ends[None, :]).astype(jnp.int32), axis=1)
    alive = (positions < ends[-1]).astype(jnp.float32)
    slots = jnp.arange(lengths.shape[0], dtype=jnp.int32)
    member = (segment[:, None] == slots[None, :]).astype(jnp.float32)
    finer = jnp.sum(member * classes[None, :].astype(jnp.float32), axis=1)
    return (segment, alive, finer)


def layer_norm(values, gain, shift):
    average = jnp.mean(values, axis=-1, keepdims=True)
    centre = values - average
    spread = jnp.mean(centre * centre, axis=-1, keepdims=True)
    return centre * lax.rsqrt(spread + EPS_NORM) * gain + shift


def gelu_exact(values):
    return jax.nn.gelu(values, approximate=False)


def masked_scores(query_block, segment_block, keys_all, segment_all, scaling):
    scores = (
        jnp.einsum("qhd,khd->hqk", query_block, keys_all, preferred_element_type=jnp.float32)
        * scaling
    )
    same = segment_block[:, None] == segment_all[None, :]
    return jnp.where(same[None], scores, NEG_BIG)


def adamw(weight, grad, first, second, clip, rate):
    scaled = grad * clip
    first_new = BETA_ONE * first + (1.0 - BETA_ONE) * scaled
    second_new = BETA_TWO * second + (1.0 - BETA_TWO) * scaled * scaled
    update = (
        first_new
        / (1.0 - BETA_ONE**STEP)
        / (jnp.sqrt(second_new / (1.0 - BETA_TWO**STEP)) + ADAM_EPS)
    )
    return (weight - rate * (update + DECAY * weight), first_new, second_new)


def transposed_dot(left, right):
    return jnp.einsum("ti,tj->ij", left, right, preferred_element_type=jnp.float32)


def body(
    pixels,
    image_tokens,
    patch_class,
    resize_coarse,
    resize_fine,
    w_base,
    w_qkv,
    w_proj,
    w_fc1,
    w_fc2,
    small_params,
    first_base,
    first_qkv,
    first_proj,
    first_fc1,
    first_fc2,
    first_small,
    second_base,
    second_qkv,
    second_proj,
    second_fc1,
    second_fc2,
    second_small,
    cotangent,
):
    bfloat = jnp.bfloat16
    rows_here = pixels.shape[0]
    block_rows = min(512, rows_here)
    block_count = rows_here // block_rows
    scaling = 1.0 / math.sqrt(HEAD_DIM)
    highest = lax.Precision.HIGHEST
    gathered = (
        lax.all_gather(w_base.astype(bfloat), "fsdp", axis=0, tiled=True),
        lax.all_gather(w_qkv.astype(bfloat), "fsdp", axis=0, tiled=True),
        lax.all_gather(w_proj.astype(bfloat), "fsdp", axis=0, tiled=True),
        lax.all_gather(w_fc1.astype(bfloat), "fsdp", axis=0, tiled=True),
        lax.all_gather(w_fc2.astype(bfloat), "fsdp", axis=0, tiled=True),
        lax.all_gather(small_params.astype(bfloat), "fsdp", axis=1, tiled=True),
    )

    def resized(weights):
        coarse = jnp.dot(resize_coarse, weights[0], preferred_element_type=jnp.float32).astype(
            bfloat
        )
        finer_w = jnp.dot(resize_fine, weights[0], preferred_element_type=jnp.float32).astype(
            bfloat
        )
        return (coarse, finer_w)

    segment, alive, finer = rows_plan(image_tokens[0], patch_class[0], rows_here)
    fine_col = finer[:, None]
    coarse_weight, fine_weight = resized(gathered)
    vectors = gathered[5].astype(jnp.float32)
    patch = jnp.dot(pixels, coarse_weight, preferred_element_type=jnp.float32) * (1.0 - fine_col)
    patch = (
        patch
        + jnp.dot(pixels[:, :PIXF], fine_weight, preferred_element_type=jnp.float32) * fine_col
    )
    state_zero = patch + vectors[0]
    normed_one = layer_norm(state_zero, vectors[1], vectors[2]).astype(bfloat)
    qkv_all = jnp.dot(normed_one, gathered[1], preferred_element_type=jnp.float32).astype(bfloat)
    queries = qkv_all[:, :D].reshape(rows_here, HEADS, HEAD_DIM)
    keys_all = qkv_all[:, D : 2 * D].reshape(rows_here, HEADS, HEAD_DIM)
    values_all = qkv_all[:, 2 * D :].reshape(rows_here, HEADS, HEAD_DIM)
    query_blocks = queries.reshape(block_count, block_rows, HEADS, HEAD_DIM)
    segment_blocks = segment.reshape(block_count, block_rows)

    def attend_step(carry, blocks):
        query_block, segment_block = blocks
        scores = masked_scores(query_block, segment_block, keys_all, segment, scaling)
        highest_score = jnp.max(scores, axis=-1, keepdims=True)
        raised = jnp.exp(scores - highest_score)
        totals = jnp.sum(raised, axis=-1, keepdims=True)
        probabilities = (raised / totals).astype(bfloat)
        mixed_block = jnp.einsum(
            "hqk,khd->qhd", probabilities, values_all, preferred_element_type=jnp.float32
        )
        return (carry, (mixed_block, (highest_score + jnp.log(totals))[..., 0]))

    _, (mixed_blocks, log_totals) = lax.scan(attend_step, None, (query_blocks, segment_blocks))
    mixed = mixed_blocks.reshape(rows_here, D).astype(bfloat)
    state_one = (
        state_zero + jnp.dot(mixed, gathered[2], preferred_element_type=jnp.float32) + vectors[3]
    )
    normed_two = layer_norm(state_one, vectors[4], vectors[5]).astype(bfloat)
    before = jnp.dot(normed_two, gathered[3], preferred_element_type=jnp.float32) + vectors[
        7:11
    ].reshape(FF)
    hidden = gelu_exact(before).astype(bfloat)
    state_two = (
        state_one + jnp.dot(hidden, gathered[4], preferred_element_type=jnp.float32) + vectors[6]
    )
    activations = (state_two * alive[:, None]).astype(bfloat)
    regathered = (
        lax.all_gather(w_base.astype(bfloat), "fsdp", axis=0, tiled=True),
        lax.all_gather(w_qkv.astype(bfloat), "fsdp", axis=0, tiled=True),
        lax.all_gather(w_proj.astype(bfloat), "fsdp", axis=0, tiled=True),
        lax.all_gather(w_fc1.astype(bfloat), "fsdp", axis=0, tiled=True),
        lax.all_gather(w_fc2.astype(bfloat), "fsdp", axis=0, tiled=True),
        lax.all_gather(small_params.astype(bfloat), "fsdp", axis=1, tiled=True),
    )
    coarse_back, fine_back = resized(regathered)
    grad_two = cotangent.astype(jnp.float32) * alive[:, None]
    grad_out_bias = jnp.sum(grad_two, axis=0)
    grad_branch = grad_two.astype(bfloat)
    grad_fc2 = transposed_dot(hidden, grad_branch)
    grad_hidden = jnp.dot(grad_branch, regathered[4].T, preferred_element_type=jnp.float32)
    _, gelu_back = jax.vjp(gelu_exact, before)
    grad_before = gelu_back(grad_hidden)[0].astype(bfloat)
    grad_fc1_bias = jnp.sum(grad_before.astype(jnp.float32), axis=0)
    grad_fc1 = transposed_dot(normed_two, grad_before)
    grad_normed_two = jnp.dot(grad_before, regathered[3].T, preferred_element_type=jnp.float32)
    _, norm_two_back = jax.vjp(layer_norm, state_one, vectors[4], vectors[5])
    grad_one_part, grad_gain_two, grad_shift_two = norm_two_back(grad_normed_two)
    grad_one = grad_two + grad_one_part
    grad_proj_bias = jnp.sum(grad_one, axis=0)
    grad_attn = grad_one.astype(bfloat)
    grad_proj = transposed_dot(mixed, grad_attn)
    grad_mixed = jnp.dot(grad_attn, regathered[2].T, preferred_element_type=jnp.float32).astype(
        bfloat
    )
    grad_mixed_blocks = grad_mixed.reshape(block_count, block_rows, HEADS, HEAD_DIM)

    def attend_back(carry, blocks):
        grad_keys, grad_values = carry
        query_block, segment_block, grad_block, log_block = blocks
        scores = masked_scores(query_block, segment_block, keys_all, segment, scaling)
        softened = jnp.exp(scores - log_block[..., None])
        probabilities = softened.astype(bfloat)
        grad_values = grad_values + jnp.einsum(
            "hqk,qhd->khd", probabilities, grad_block, preferred_element_type=jnp.float32
        )
        grad_probs = jnp.einsum(
            "qhd,khd->hqk", grad_block, values_all, preferred_element_type=jnp.float32
        )
        grad_scores = softened * (
            grad_probs - jnp.sum(grad_probs * softened, axis=-1, keepdims=True)
        )
        grad_scores = grad_scores.astype(bfloat)
        grad_query = (
            jnp.einsum("hqk,khd->qhd", grad_scores, keys_all, preferred_element_type=jnp.float32)
            * scaling
        )
        grad_keys = (
            grad_keys
            + jnp.einsum(
                "hqk,qhd->khd", grad_scores, query_block, preferred_element_type=jnp.float32
            )
            * scaling
        )
        return ((grad_keys, grad_values), grad_query)

    zeros_heads = jnp.zeros((rows_here, HEADS, HEAD_DIM), jnp.float32)
    (grad_keys, grad_values), grad_queries = lax.scan(
        attend_back,
        (zeros_heads, zeros_heads),
        (query_blocks, segment_blocks, grad_mixed_blocks, log_totals),
    )
    grad_qkv_all = jnp.concatenate(
        [
            grad_queries.reshape(rows_here, D),
            grad_keys.reshape(rows_here, D),
            grad_values.reshape(rows_here, D),
        ],
        axis=1,
    ).astype(bfloat)
    grad_qkv = transposed_dot(normed_one, grad_qkv_all)
    grad_normed_one = jnp.dot(grad_qkv_all, regathered[1].T, preferred_element_type=jnp.float32)
    _, norm_one_back = jax.vjp(layer_norm, state_zero, vectors[1], vectors[2])
    grad_zero_part, grad_gain_one, grad_shift_one = norm_one_back(grad_normed_one)
    grad_zero = grad_one + grad_zero_part
    grad_embed_bias = jnp.sum(grad_zero, axis=0)
    grad_patch = grad_zero.astype(bfloat)
    grad_coarse_rows = grad_patch * (1.0 - fine_col).astype(bfloat)
    grad_fine_rows = grad_patch * fine_col.astype(bfloat)
    grad_coarse = transposed_dot(pixels, grad_coarse_rows)
    grad_fine = transposed_dot(pixels[:, :PIXF], grad_fine_rows)
    pixel_grad = jnp.dot(grad_coarse_rows, coarse_back.T, preferred_element_type=jnp.float32)
    fine_pixels = jnp.dot(grad_fine_rows, fine_back.T, preferred_element_type=jnp.float32)
    pixel_grad = (pixel_grad + jnp.pad(fine_pixels, ((0, 0), (0, PIXC - PIXF)))).astype(bfloat)
    grad_small = jnp.concatenate(
        [
            jnp.stack(
                [
                    grad_embed_bias,
                    grad_gain_one,
                    grad_shift_one,
                    grad_proj_bias,
                    grad_gain_two,
                    grad_shift_two,
                    grad_out_bias,
                ]
            ),
            grad_fc1_bias.reshape(4, D),
        ],
        axis=0,
    )
    grad_base = jnp.dot(resize_coarse.astype(jnp.float32).T, grad_coarse, precision=highest)
    grad_base = grad_base + jnp.dot(resize_fine.astype(jnp.float32).T, grad_fine, precision=highest)
    shards = (
        lax.psum_scatter(grad_base, "fsdp", scatter_dimension=0, tiled=True),
        lax.psum_scatter(grad_qkv, "fsdp", scatter_dimension=0, tiled=True),
        lax.psum_scatter(grad_proj, "fsdp", scatter_dimension=0, tiled=True),
        lax.psum_scatter(grad_fc1, "fsdp", scatter_dimension=0, tiled=True),
        lax.psum_scatter(grad_fc2, "fsdp", scatter_dimension=0, tiled=True),
        lax.psum_scatter(grad_small, "fsdp", scatter_dimension=1, tiled=True),
    )
    shards = (
        lax.psum(shards[0].astype(jnp.bfloat16), "rep").astype(jnp.float32),
        lax.psum(shards[1].astype(jnp.bfloat16), "rep").astype(jnp.float32),
        lax.psum(shards[2].astype(jnp.bfloat16), "rep").astype(jnp.float32),
        lax.psum(shards[3].astype(jnp.bfloat16), "rep").astype(jnp.float32),
        lax.psum(shards[4].astype(jnp.bfloat16), "rep").astype(jnp.float32),
        lax.psum(shards[5].astype(jnp.bfloat16), "rep").astype(jnp.float32),
    )
    squares = jnp.float32(0.0)
    for shard in shards:
        squares = squares + jnp.sum(shard * shard)
    grad_norm = jnp.sqrt(lax.psum(squares, "fsdp"))
    clip = jnp.minimum(1.0, CLIP_NORM / grad_norm)
    masters = (w_base, w_qkv, w_proj, w_fc1, w_fc2, small_params)
    firsts = (first_base, first_qkv, first_proj, first_fc1, first_fc2, first_small)
    seconds = (second_base, second_qkv, second_proj, second_fc1, second_fc2, second_small)
    rates = (RATE, RATE, RATE, RATE, RATE, RATE_SMALL)
    results = [
        adamw(masters[index], shards[index], firsts[index], seconds[index], clip, rates[index])
        for index in range(6)
    ]
    return (
        activations,
        pixel_grad,
        grad_norm,
        results[0][0],
        results[1][0],
        results[2][0],
        results[3][0],
        results[4][0],
        results[5][0],
        results[0][1],
        results[1][1],
        results[2][1],
        results[3][1],
        results[4][1],
        results[5][1],
        results[0][2],
        results[1][2],
        results[2][2],
        results[3][2],
        results[4][2],
        results[5][2],
    )


def solution(mesh):
    in_specs = (
        P(("fsdp", "rep"), None),
        P(("fsdp", "rep"), None),
        P(("fsdp", "rep"), None),
        P(),
        P(),
        P("fsdp", None),
        P("fsdp", None),
        P("fsdp", None),
        P("fsdp", None),
        P("fsdp", None),
        P(None, "fsdp"),
        P("fsdp", None),
        P("fsdp", None),
        P("fsdp", None),
        P("fsdp", None),
        P("fsdp", None),
        P(None, "fsdp"),
        P("fsdp", None),
        P("fsdp", None),
        P("fsdp", None),
        P("fsdp", None),
        P("fsdp", None),
        P(None, "fsdp"),
        P(("fsdp", "rep"), None),
    )
    out_specs = (
        P(("fsdp", "rep"), None),
        P(("fsdp", "rep"), None),
        P(),
        P("fsdp", None),
        P("fsdp", None),
        P("fsdp", None),
        P("fsdp", None),
        P("fsdp", None),
        P(None, "fsdp"),
        P("fsdp", None),
        P("fsdp", None),
        P("fsdp", None),
        P("fsdp", None),
        P("fsdp", None),
        P(None, "fsdp"),
        P("fsdp", None),
        P("fsdp", None),
        P("fsdp", None),
        P("fsdp", None),
        P("fsdp", None),
        P(None, "fsdp"),
    )
    return jax.shard_map(body, mesh=mesh, in_specs=in_specs, out_specs=out_specs, check_vma=False)
```

profile of v0, /device:TPU:0, one launch (start us, length us, event | category | flops | bytes accessed | tf_op | source)
XLA Modules:
  0.0 1137.4 jit_solution(5933741198364143975)
XLA Ops:
  15.5 23.4 %all-gather = bf16[16,48,11]{1,2,0:T(8,128)(2,1)S(1)} all-gather(bf16[1,48,11]{1,2,0:T(8,128)(2,1)S(1)} %convert_bitcast_fusion), channel_id=1, replica_groups=mesh['fsdp'=16,'rep'=2] {'fsdp'}, dimensions={0}, use_global_device_ids=true | all-gather | bytes 17952 | tf_op jit(solution)/shard_map/all_gather | solution.py:113
  44.8 22.5 %all-gather.7.cloned.1.call-done = bf16[3072,768]{1,0:T(8,128)(2,1)} async-done(((bf16[192,768]{1,0:T(8,128)(2,1)}), bf16[3072,768]{1,0:T(8,128)(2,1)}) %all-gather.7.cloned.1.call-update) | async-done | bytes 4718608 | tf_op jit(solution)/shard_map/all_gather | solution.py:108
  82.5 33.4 %all-gather.9.cloned.1.call-done = bf16[768,2304]{1,0:T(8,128)(2,1)} async-done(((bf16[48,2304]{1,0:T(8,128)(2,1)}), bf16[768,2304]{1,0:T(8,128)(2,1)}) %all-gather.9.cloned.1.call-update) | async-done | bytes 3538960 | tf_op jit(solution)/shard_map/all_gather | solution.py:109
  139.2 74.0 %while.27 = (s32[]{:T(128)}, bf16[2,512,12,64]{1,3,2,0:T(8,128)(2,1)}, f32[2,12,512]{2,1,0:T(8,128)S(1)}, s32[2,512]{1,0:T(2,128)S(1)}, s32[1024]{0:T(1024)S(1)}...) while((s32[]{:T(128)}, ...), condition=%wide.region_8.9_spmd, body=%wide.region_5.8_spmd.sunk | while | flops 1686628352 | bytes 190286000 | solution.py:155
  139.5 12.2 %fusion.169 = (f32[12,512]{1,0:T(8,128)S(1)}, f32[12,512,1024]{2,1,0:T(8,128)}) fusion(pred[512,1024]{1,0:T(8,128)(4,1)S(1)} %broadcast_compare_fusion.4, bf16[1024,12,64]{0,2,1:T(8,128)(2,1)S(1)} %get-tuple-element.617, bf16[2,512,12,64]{1,3,2,0:T(8,128)(2,1)} %get-tuple-element.616, s32[]{:T(128)S(6)} %copy.225), kind=kOutput, calls=%fused_computation.3.clone.1 | convolution fusion | flops 824174592 | bytes 28073988 | tf_op jit(solution)/shard_map/while/body/eval_jaxpr/qhd,khd->hqk/dot_general | solution.py:52
  151.7 12.3 %fusion.170 = f32[12,512]{1,0:T(8,128)S(1)} fusion(f32[12,512,1024]{2,1,0:T(8,128)} %get-tuple-element.578, f32[12,512]{1,0:T(8,128)S(1)} %get-tuple-element.579, pred[512,1024]{1,0:T(8,128)(4,1)S(1)} %broadcast_compare_fusion.4), kind=kLoop, calls=%fused_computation.4.clone.1 | loop fusion | flops 25159680 | bytes 25739264 | tf_op jit(solution)/shard_map/while/body/eval_jaxpr/reduce_sum | solution.py:148
  176.4 12.5 %fusion.169 = (f32[12,512]{1,0:T(8,128)S(1)}, f32[12,512,1024]{2,1,0:T(8,128)}) fusion(pred[512,1024]{1,0:T(8,128)(4,1)S(1)} %broadcast_compare_fusion.4, bf16[1024,12,64]{0,2,1:T(8,128)(2,1)S(1)} %get-tuple-element.617, bf16[2,512,12,64]{1,3,2,0:T(8,128)(2,1)} %get-tuple-element.616, s32[]{:T(128)S(6)} %copy.225), kind=kOutput, calls=%fused_computation.3.clone.1 | convolution fusion | flops 824174592 | bytes 28073988 | tf_op jit(solution)/shard_map/while/body/eval_jaxpr/qhd,khd->hqk/dot_general | solution.py:52
  188.9 12.4 %fusion.170 = f32[12,512]{1,0:T(8,128)S(1)} fusion(f32[12,512,1024]{2,1,0:T(8,128)} %get-tuple-element.578, f32[12,512]{1,0:T(8,128)S(1)} %get-tuple-element.579, pred[512,1024]{1,0:T(8,128)(4,1)S(1)} %broadcast_compare_fusion.4), kind=kLoop, calls=%fused_computation.4.clone.1 | loop fusion | flops 25159680 | bytes 25739264 | tf_op jit(solution)/shard_map/while/body/eval_jaxpr/reduce_sum | solution.py:148
  224.5 38.2 %multiply_convert_fusion.1 = (bf16[1024,3072]{1,0:T(8,128)(2,1)}, f32[1024,3072]{1,0:T(8,128)}, f32[1024,3072]{1,0:T(8,128)}) fusion(f32[3072]{0:T(1024)S(1)} %copy-done.59, bf16[768,3072]{1,0:T(8,128)(2,1)} %all-gather.13.cloned.1.call-done, f32[1024,768]{0,1:T(8,128)} %copy-done.4, f32[768]{0:T(1024)S(1)} %copy-done.61, f32[768]{0:T(1024)S(1)} %copy-done.40, ...), kind=kOutput, calls=%fused_computation.48 | convolution fusion | flops 5043388416 | bytes 39348224 | tf_op jit(solution)/shard_map/dot_general | solution.py:161
  265.6 19.1 %convert_reduce_fusion = (f32[3072]{0:T(1024)}, bf16[1024,3072]{1,0:T(8,128)(2,1)}) fusion(f32[1024,3072]{1,0:T(8,128)} %get-tuple-element.441, bf16[3072,768]{1,0:T(8,128)(2,1)} %all-gather.15.cloned.1.call-done, bf16[1024,768]{0,1:T(8,128)(2,1)} %copy.181, f32[1024]{0:T(1024)S(1)} %copy-done.56, f32[1024,3072]{1,0:T(8,128)} %get-tuple-element.459, ...), kind=kOutput, calls=%fused_computation.46 | convolution fusion | flops 4887671808 | bytes 37777408 | tf_op jit(solution)/shard_map/dot_general | solution.py:182
  327.3 168.9 %while.28 = (s32[]{:T(128)}, f32[1024,12,64]{0,2,1:T(8,128)}, f32[1024,12,64]{0,2,1:T(8,128)}, bf16[2,512,12,64]{1,3,2,0:T(8,128)(2,1)}, bf16[2,512,12,64]{1,3,2...) while((s32[]{:T(128)}, f32[1024,12,64]{0,2,1:T(8,128)}, ...), condition=%wide.region_15.16_spmd.clone, body=%wide.region_13.15_spmd.clone.sunk | while | flops 4125747200 | bytes 219343024 | solution.py:229
  340.0 13.8 %bitcast_add_fusion.6 = f32[1024,12,64]{0,2,1:T(8,128)} fusion(f32[1024,12,64]{0,2,1:T(8,128)} %get-tuple-element.635, f32[12,512,1024]{2,1,0:T(8,128)} %fusion.180, f32[12,512]{1,0:T(8,128)S(1)} %dynamic-slice_bitcast_fusion.2, pred[512,1024]{1,0:T(8,128)(4,1)S(1)} %broadcast_compare_fusion.5, pred[]{:T(512)S(6)} %compare.4, ...), kind=kOutput, calls=%fused_computation.22.clone.1 | convolution fusion | flops 832045056 | bytes 32800772 | tf_op jit(solution)/shard_map/while/body/eval_jaxpr/hqk,qhd->khd/dot_general | solution.py:205
  353.8 18.1 %multiply_reduce_fusion.8 = (f32[12,512]{1,0:T(8,128)S(1)}, f32[12,512,1024]{2,1,0:T(8,128)}) fusion(f32[12,512,1024]{2,1,0:T(8,128)} %fusion.180, f32[12,512]{1,0:T(8,128)S(1)} %dynamic-slice_bitcast_fusion.2, pred[512,1024]{1,0:T(8,128)(4,1)S(1)} %broadcast_compare_fusion.5, bf16[1024,12,64]{0,2,1:T(8,128)(2,1)} %get-tuple-element.656, ...), kind=kOutput, calls=%fused_computation.17.clone.1 | convolution fusion | flops 836757504 | bytes 53264388 | tf_op jit(solution)/shard_map/while/body/eval_jaxpr/qhd,khd->hqk/dot_general | solution.py:208
  371.9 21.5 %multiply_convert_fusion.4 = bf16[12,512,1024]{2,1,0:T(8,128)(2,1)} fusion(f32[12,512,1024]{2,1,0:T(8,128)} %get-tuple-element.591, f32[12,512,1024]{2,1,0:T(8,128)} %fusion.180, f32[12,512]{1,0:T(8,128)S(1)} %get-tuple-element.592, f32[12,512]{1,0:T(8,128)S(1)} %dynamic-slice_bitcast_fusion.2, pred[512,1024]{1,0:T(8,128)(4,1)S(1)} %broadcast_compare_fusion.5), kind=kLoop, calls=%fused_computation.16.clone.1 | loop fusion | flops 37748736 | bytes 63488000 | tf_op jit(solution)/shard_map/while/body/eval_jaxpr/convert_element_type | solution.py:214
  423.4 14.4 %bitcast_add_fusion.6 = f32[1024,12,64]{0,2,1:T(8,128)} fusion(f32[1024,12,64]{0,2,1:T(8,128)} %get-tuple-element.635, f32[12,512,1024]{2,1,0:T(8,128)} %fusion.180, f32[12,512]{1,0:T(8,128)S(1)} %dynamic-slice_bitcast_fusion.2, pred[512,1024]{1,0:T(8,128)(4,1)S(1)} %broadcast_compare_fusion.5, pred[]{:T(512)S(6)} %compare.4, ...), kind=kOutput, calls=%fused_computation.22.clone.1 | convolution fusion | flops 832045056 | bytes 32800772 | tf_op jit(solution)/shard_map/while/body/eval_jaxpr/hqk,qhd->khd/dot_general | solution.py:205
  437.8 18.1 %multiply_reduce_fusion.8 = (f32[12,512]{1,0:T(8,128)S(1)}, f32[12,512,1024]{2,1,0:T(8,128)}) fusion(f32[12,512,1024]{2,1,0:T(8,128)} %fusion.180, f32[12,512]{1,0:T(8,128)S(1)} %dynamic-slice_bitcast_fusion.2, pred[512,1024]{1,0:T(8,128)(4,1)S(1)} %broadcast_compare_fusion.5, bf16[1024,12,64]{0,2,1:T(8,128)(2,1)} %get-tuple-element.656, ...), kind=kOutput, calls=%fused_computation.17.clone.1 | convolution fusion | flops 836757504 | bytes 53264388 | tf_op jit(solution)/shard_map/while/body/eval_jaxpr/qhd,khd->hqk/dot_general | solution.py:208
  455.8 21.2 %multiply_convert_fusion.4 = bf16[12,512,1024]{2,1,0:T(8,128)(2,1)} fusion(f32[12,512,1024]{2,1,0:T(8,128)} %get-tuple-element.591, f32[12,512,1024]{2,1,0:T(8,128)} %fusion.180, f32[12,512]{1,0:T(8,128)S(1)} %get-tuple-element.592, f32[12,512]{1,0:T(8,128)S(1)} %dynamic-slice_bitcast_fusion.2, pred[512,1024]{1,0:T(8,128)(4,1)S(1)} %broadcast_compare_fusion.5), kind=kLoop, calls=%fused_computation.16.clone.1 | loop fusion | flops 37748736 | bytes 63488000 | tf_op jit(solution)/shard_map/while/body/eval_jaxpr/convert_element_type | solution.py:214
  524.2 12.7 %fusion.49 = f32[3072,768]{1,0:T(8,128)} fusion(bf16[1024,3072]{1,0:T(8,128)(2,1)} %get-tuple-element.440, bf16[1024,768]{0,1:T(8,128)(2,1)S(1)} %copy-done.15, f32[1024]{0:T(1024)S(1)} %copy-done.57), kind=kOutput, calls=%fused_computation.97 | convolution fusion | flops 4834197504 | bytes 17305600
  603.3 112.8 %reduce-scatter.17.cloned.1.call-done = f32[48,3072]{1,0:T(8,128)} async-done(((f32[768,3072]{1,0:T(8,128)}), f32[48,3072]{1,0:T(8,128)}) %reduce-scatter.17.cloned.1.call-update) | async-done | bytes 589840 | tf_op jit(solution)/shard_map/reduce_scatter | solution.py:279
  717.9 114.0 %reduce-scatter.21.cloned.1.call-done = f32[192,768]{1,0:T(8,128)} async-done(((f32[3072,768]{1,0:T(8,128)}), f32[192,768]{1,0:T(8,128)}) %reduce-scatter.21.cloned.1.call-update) | async-done | bytes 589840
  833.8 113.1 %reduce-scatter.19.cloned.1.call-done = f32[192,768]{1,0:T(8,128)} async-done(((f32[3072,768]{1,0:T(8,128)}), f32[192,768]{1,0:T(8,128)}) %reduce-scatter.19.cloned.1.call-update) | async-done | bytes 589840
  963.0 43.7 %reduce-scatter.23.cloned.1.call-done = f32[48,11]{1,0:T(8,128)} async-done(((f32[768,11]{1,0:T(8,128)}), f32[48,11]{1,0:T(8,128)}) %reduce-scatter.23.cloned.1.call-update) | async-done | bytes 2128
  1013.1 44.2 %all-reduce.4.cloned.1.call-done = (bf16[192,768]{0,1:T(8,128)(2,1)}, bf16[48,2304]{1,0:T(8,128)(2,1)}, bf16[48,768]{1,0:T(8,128)(2,1)}, bf16[48,3072]{1,0:T(8,128)(2,1)}, bf16[192,768]{0,1:T(8,128)(2,1)}) async-done(((bf16[192,768]{0,1:T(8,128)(2,1)}, bf16[48,2304]{1,0:T(8,128)(2,1)}, bf16[48,768]{1,0:T(8,128)(2,1)}, bf16[48,3072]{1,0:T(8,128)(2,1)}, bf16[192,768]{0,1:T(8,128)(2,1)}), ...) | async-done | bytes 1179664 | tf_op jit(solution)/shard_map/psum | solution.py:284
  1072.5 33.6 %psum.55 = f32[]{:T(128)} all-reduce(f32[]{:T(128)S(6)} %add.297), channel_id=1, replica_groups=mesh['fsdp'=16,'rep'=2] {'fsdp'}, use_global_device_ids=true, to_apply=%region_44.45 | all-reduce | flops 1 | bytes 8 | tf_op jit(solution)/shard_map/psum | solution.py:294
  (327 shorter events, 348.4 us)
Async XLA Ops:
  7.2 60.1 %copy-start = (bf16[192,3072]{1,0:T(8,128)(2,1)S(1)}, bf16[192,3072]{1,0:T(8,128)(2,1)}, u32[]{:S(2)}) copy-start(bf16[192,3072]{1,0:T(8,128)(2,1)} %param.32) | copy-start | bytes 3538948
  7.2 33.2 %copy-start.71 = (s32[1,4]{1,0:T(1,128)S(1)}, s32[1,4]{1,0:T(1,128)}, u32[]{:S(2)}) copy-start(s32[1,4]{1,0:T(1,128)} %param.30) | copy-start | bytes 52
  7.3 35.9 %copy-start.23 = (bf16[1024,768]{1,0:T(8,128)(2,1)S(1)}, bf16[1024,768]{1,0:T(8,128)(2,1)}, u32[]{:S(2)}) copy-start(bf16[1024,768]{1,0:T(8,128)(2,1)} %param.51) | copy-start | bytes 4718596
  7.3 60.0 %all-gather.7.cloned.1.call-start = ((), (), s32[]{:S(2)}) async-start(), calls=%async_computation.6 | async-start | bytes 5013504 | tf_op jit(solution)/shard_map/all_gather | solution.py:108
  9.3 106.6 %all-gather.9.cloned.1.call-start = ((), (), s32[]{:S(2)}) async-start(), calls=%async_computation.7 | async-start | bytes 3760128 | tf_op jit(solution)/shard_map/all_gather | solution.py:109
  11.1 206.7 %all-gather.11.cloned.1.call-start = ((), (), s32[]{:S(2)}) async-start(), calls=%async_computation.8 | async-start | bytes 1253376 | tf_op jit(solution)/shard_map/all_gather | solution.py:110
  12.7 211.7 %all-gather.13.cloned.1.call-start = ((), (), s32[]{:S(2)}) async-start(), calls=%async_computation.9 | async-start | bytes 5013504 | tf_op jit(solution)/shard_map/all_gather | solution.py:111
  14.6 251.0 %all-gather.15.cloned.1.call-start = ((), (), s32[]{:S(2)}) async-start(), calls=%async_computation.10 | async-start | bytes 5013504 | tf_op jit(solution)/shard_map/all_gather | solution.py:112
  15.4 584.5 %reduce-scatter.15.cloned.1.call-start = ((), (), s32[]{:S(2)}) async-start(), calls=%async_computation.12 | async-start | bytes 2506752 | tf_op jit(solution)/shard_map/reduce_scatter | solution.py:278
  39.7 76.2 %copy-start.48 = (f32[768]{0:T(1024)}, f32[768]{0:T(1024)S(1)}, u32[]{:S(2)}) copy-start(f32[768]{0:T(1024)S(1)} %get-tuple-element.375) | copy-start | bytes 9220
  39.7 76.2 %copy-start.63 = (f32[768]{0:T(1024)}, f32[768]{0:T(1024)S(1)}, u32[]{:S(2)}) copy-start(f32[768]{0:T(1024)S(1)} %get-tuple-element.374) | copy-start | bytes 9220
  80.4 35.5 %copy-start.42 = (f32[1024]{0:T(1024)}, f32[1024]{0:T(1024)S(1)}, u32[]{:S(2)}) copy-start(f32[1024]{0:T(1024)S(1)} %broadcast_multiply_fusion.1) | copy-start | bytes 12292
  82.5 33.4 %copy-start.46 = (f32[1024]{0:T(1024)}, f32[1024]{0:T(1024)S(1)}, u32[]{:S(2)}) copy-start(f32[1024]{0:T(1024)S(1)} %multiply_reduce_fusion.6) | copy-start | bytes 12292
  82.5 33.4 %copy-start.50 = (f32[1024]{0:T(1024)}, f32[1024]{0:T(1024)S(1)}, u32[]{:S(2)}) copy-start(f32[1024]{0:T(1024)S(1)} %fusion.89) | copy-start | bytes 12292
  222.4 82.8 %copy-start.38 = (f32[1024]{0:T(1024)}, f32[1024]{0:T(1024)S(1)}, u32[]{:S(2)}) copy-start(f32[1024]{0:T(1024)S(1)} %broadcast_multiply_fusion) | copy-start | bytes 12292
  224.4 80.8 %copy-start.44 = (f32[1024]{0:T(1024)}, f32[1024]{0:T(1024)S(1)}, u32[]{:S(2)}) copy-start(f32[1024]{0:T(1024)S(1)} %fusion.90) | copy-start | bytes 12292
  224.5 41.1 %copy-start.56 = (f32[1024]{0:T(1024)S(1)}, f32[1024]{0:T(1024)}, u32[]{:S(2)}) copy-start(f32[1024]{0:T(1024)} %fusion.88) | copy-start | bytes 12292
  326.0 275.6 %reduce-scatter.13.cloned.1.call-start = ((), (), s32[]{:S(2)}) async-start(), calls=%async_computation.11 | async-start | bytes 7520256 | tf_op jit(solution)/shard_map/reduce_scatter | solution.py:277
  511.3 204.7 %reduce-scatter.17.cloned.1.call-start = ((), (), s32[]{:S(2)}) async-start(), calls=%async_computation.13 | async-start | bytes 10027008 | tf_op jit(solution)/shard_map/reduce_scatter | solution.py:279
  522.6 309.2 %reduce-scatter.21.cloned.1.call-start = ((), (), s32[]{:S(2)}) async-start(), calls=%async_computation.15 | async-start | bytes 10027008
  536.9 410.0 %reduce-scatter.19.cloned.1.call-start = ((), (), s32[]{:S(2)}) async-start(), calls=%async_computation.14 | async-start | bytes 10027008
  589.5 417.2 %reduce-scatter.23.cloned.1.call-start = ((), (), s32[]{:S(2)}) async-start(), calls=%async_computation.16 | async-start | bytes 417792
  591.4 465.9 %all-reduce.4.cloned.1.call-start = ((), (), s32[]{:S(2)}) async-start(), calls=%async_computation.17 | async-start | bytes 2752512 | tf_op jit(solution)/shard_map/psum | solution.py:284
  597.8 351.1 %copy-start.60 = (f32[768]{0:T(1024)S(1)}, f32[768]{0:T(1024)}, u32[]{:S(2)}) copy-start(f32[768]{0:T(1024)} %get-tuple-element.370) | copy-start | bytes 9220
  (67 other events, 370.3 us)
Sparse Core Ops, SparseCore 0:
  11.0 56.2 all-gather.6
  70.1 45.7 all-gather.8
  118.8 37.3 all-gather.10
  158.8 52.1 all-gather.12
  213.8 51.7 all-gather.14
  326.1 61.4 reduce-scatter.14
  511.5 89.5 reduce-scatter.12
  605.2 110.8 reduce-scatter.16
  720.7 111.0 reduce-scatter.20
  835.8 111.0 reduce-scatter.18
  951.4 55.3 reduce-scatter.22
  1010.3 46.9 all-reduce.3
where the time goes:
time: 1150 us; the launch traced here: 1140 us
  waiting for transfers between devices  487 us (42%)
  matrix products  339 us (29%)
  other arithmetic  122 us (11%)
  local copies, waits for them, and re-layouts  106 us (9%)
  blocking collectives  62 us (5%)
  between operations  21.1 us (2%)
    unnamed x15, waiting for transfers between devices  271 us
    reduce_scatter x1, waiting for transfers between devices, body(): lax.psum_scatter(grad_fc1, 'fsdp', scatter_dimension=0, tiled=True)  113 us
    unnamed x168, local copies, waits for them, and re-layouts  59.1 us
    dot_general x4, matrix products, masked_scores(): jnp.einsum('qhd,khd->hqk', query_block, keys_all, preferred_element_type=...  48 us
    psum x1, waiting for transfers between devices, body(): lax.psum(shards[0].astype(jnp.bfloat16), 'rep').astype(jnp.float32)  44.2 us
    convert_element_type x2, other arithmetic, attend_back(): grad_scores = grad_scores.astype(bfloat)  42.7 us
    dot_general x1, matrix products, body(): jnp.dot(normed_two, gathered[3], preferred_element_type=jnp.float32)  38.2 us
    dot_general x2, matrix products, attend_back(): jnp.einsum('qhd,khd->hqk', grad_block, values_all, preferred_element_type...  36.1 us
  transfers between devices with their start and end apart: 12, of which 8 were waited for; matrix products, arithmetic and copies ran while one was open for 40% of the time, Pallas kernels for 0%

commit v1 on v0

v1 whole, which is shorter than its diff:
```python
import functools
import math

import jax
import jax.numpy as jnp
from jax import lax
from jax.experimental import pallas as pl
from jax.experimental.pallas import tpu as pltpu
from jax.sharding import PartitionSpec as P

D = 768
HEADS = 12
HEAD_DIM = 64
FF = 3072
PIXC = 768
PIXF = 192
STEP = 10
SLOTS = 5


EPS_NORM = 1e-06
RATE = 0.05
RATE_SMALL = 0.5
BETA_ONE = 0.9
BETA_TWO = 0.95
ADAM_EPS = 1e-08
DECAY = 0.05
CLIP_NORM = 1.0


def rows_plan(lengths, classes, count):
    ends = jnp.cumsum(lengths)
    positions = jnp.arange(count, dtype=jnp.int32)
    segment = jnp.sum((positions[:, None] >= ends[None, :]).astype(jnp.int32), axis=1)
    alive = (positions < ends[-1]).astype(jnp.float32)
    slots = jnp.arange(lengths.shape[0], dtype=jnp.int32)
    member = (segment[:, None] == slots[None, :]).astype(jnp.float32)
    finer = jnp.sum(member * classes[None, :].astype(jnp.float32), axis=1)
    return (segment, alive, finer)


def layer_norm(values, gain, shift):
    average = jnp.mean(values, axis=-1, keepdims=True)
    centre = values - average
    spread = jnp.mean(centre * centre, axis=-1, keepdims=True)
    return centre * lax.rsqrt(spread + EPS_NORM) * gain + shift


def gelu_exact(values):
    return jax.nn.gelu(values, approximate=False)


LOG2E = math.log2(math.e)
FAR = -1e30
ATT_ROWS = 512


def lane_plan(rows, side, seg):
    lane = lax.broadcasted_iota(jnp.int32, (rows, 2 * HEAD_DIM), 1)
    mine = (lane < HEAD_DIM) if side == 0 else (lane >= HEAD_DIM)
    first = HEAD_DIM if side == 0 else 0
    hot = lane - first == seg
    slots = (lane >= first) & (lane < first + SLOTS)
    return lane, mine, hot, slots


def attend_kernel(seg_ref, q_ref, k_ref, v_ref, mixed_ref, log_ref, *, step):
    pair = pl.program_id(0)
    rows = q_ref.shape[0]
    seg = seg_ref[...]
    one = jnp.ones((), jnp.bfloat16)
    logs = jnp.where(pair == 0, 0.0, log_ref[...])
    outs = []
    for side in range(2):
        lane, mine, hot, slots = lane_plan(rows, side, seg)
        keys = jnp.where(
            mine, k_ref[...], jnp.where(slots & ~hot, FAR, 0.0).astype(jnp.bfloat16)
        )
        values = jnp.where(mine, v_ref[...], one)
        queries = jnp.where(mine, q_ref[...] * jnp.bfloat16(0.125), hot.astype(jnp.bfloat16))
        parts, part_logs = [], []
        for at in range(0, rows, step):
            scores = lax.dot_general(
                queries[at : at + step],
                keys,
                (((1,), (1,)), ((), ())),
                preferred_element_type=jnp.float32,
            )
            top = jnp.max(scores, axis=1, keepdims=True) * LOG2E
            raised = jnp.exp2(scores * LOG2E - top).astype(jnp.bfloat16)
            sums = jnp.dot(raised, values, preferred_element_type=jnp.float32)
            turned = pltpu.roll(sums, HEAD_DIM, 1)
            inside = mine[at : at + step]
            parts.append(sums / turned)
            part_logs.append(top + jnp.log2(jnp.where(inside, turned, sums)))
        outs.append(jnp.concatenate(parts, axis=0))
        logs = jnp.where(lane == 2 * pair + side, jnp.concatenate(part_logs, axis=0), logs)
    lane = lax.broadcasted_iota(jnp.int32, (rows, 2 * HEAD_DIM), 1)
    mixed_ref[...] = jnp.where(lane < HEAD_DIM, outs[0], outs[1]).astype(jnp.bfloat16)
    log_ref[...] = logs


def attend(qkv, seg):
    rows = qkv.shape[0]
    wide = 2 * HEAD_DIM
    pairs = D // wide
    step = min(ATT_ROWS, rows)

    def block(first):
        return pl.BlockSpec((rows, wide), lambda pair: (0, first + pair))

    return pl.pallas_call(
        functools.partial(attend_kernel, step=step),
        grid=(pairs,),
        in_specs=[
            pl.BlockSpec((rows, 1), lambda pair: (0, 0)),
            block(0),
            block(pairs),
            block(2 * pairs),
        ],
        out_specs=[block(0), pl.BlockSpec((rows, wide), lambda pair: (0, 0))],
        out_shape=[
            jax.ShapeDtypeStruct((rows, D), jnp.bfloat16),
            jax.ShapeDtypeStruct((rows, wide), jnp.float32),
        ],
        compiler_params=pltpu.CompilerParams(vmem_limit_bytes=48 * 2**20),
        cost_estimate=pl.CostEstimate(
            flops=16 * rows * rows * D,
            bytes_accessed=rows * D * 8,
            transcendentals=HEADS * rows * rows,
        ),
    )(seg, qkv, qkv, qkv)


def attend_back_kernel(
    seg_ref, q_ref, k_ref, v_ref, mixed_ref, grad_ref, log_ref, dq_ref, dk_ref, dv_ref, *, step
):
    pair = pl.program_id(0)
    rows = q_ref.shape[0]
    seg = seg_ref[...]
    zero = jnp.zeros((), jnp.bfloat16)
    product = grad_ref[...].astype(jnp.float32) * mixed_ref[...].astype(jnp.float32)
    plain_keys = k_ref[...]
    values = v_ref[...]
    scaled = q_ref[...] * jnp.bfloat16(0.125)
    results = []
    for side in range(2):
        lane, mine, hot, slots = lane_plan(rows, side, seg)
        keys = jnp.where(
            mine, plain_keys, jnp.where(slots & ~hot, FAR, 0.0).astype(jnp.bfloat16)
        )
        queries = jnp.where(mine, scaled, hot.astype(jnp.bfloat16))
        grads = jnp.where(mine, grad_ref[...], zero)
        queries_t = jnp.where(mine, scaled, zero).T
        grads_t = grads.T
        drop = jnp.sum(jnp.where(mine, product, 0.0), axis=1, keepdims=True)
        logs = jnp.sum(
            jnp.where(lane == 2 * pair + side, log_ref[...], 0.0), axis=1, keepdims=True
        )
        dq_parts, dk_t, dv_t = [], 0.0, 0.0
        for at in range(0, rows, step):
            part = slice(at, at + step)
            scores = lax.dot_general(
                queries[part],
                keys,
                (((1,), (1,)), ((), ())),
                preferred_element_type=jnp.float32,
            )
            probs = jnp.exp2(scores * LOG2E - logs[part])
            grad_probs = lax.dot_general(
                grads[part],
                values,
                (((1,), (1,)), ((), ())),
                preferred_element_type=jnp.float32,
            )
            grad_scores = (probs * (grad_probs - drop[part])).astype(jnp.bfloat16)
            probs = probs.astype(jnp.bfloat16)
            dq_parts.append(jnp.dot(grad_scores, plain_keys, preferred_element_type=jnp.float32))
            dv_t = dv_t + jnp.dot(grads_t[:, part], probs, preferred_element_type=jnp.float32)
            dk_t = dk_t + jnp.dot(
                queries_t[:, part], grad_scores, preferred_element_type=jnp.float32
            )
        results.append((jnp.concatenate(dq_parts, axis=0) * 0.125, dk_t.T, dv_t.T))
    lane = lax.broadcasted_iota(jnp.int32, (rows, 2 * HEAD_DIM), 1)
    for ref, low, high in zip((dq_ref, dk_ref, dv_ref), results[0], results[1]):
        ref[...] = jnp.where(lane < HEAD_DIM, low, high).astype(jnp.bfloat16)


def attend_back(qkv, seg, mixed, grad_mixed, logs):
    rows = qkv.shape[0]
    wide = 2 * HEAD_DIM
    pairs = D // wide
    step = min(ATT_ROWS, rows)

    def block(first):
        return pl.BlockSpec((rows, wide), lambda pair: (0, first + pair))

    return pl.pallas_call(
        functools.partial(attend_back_kernel, step=step),
        grid=(pairs,),
        in_specs=[
            pl.BlockSpec((rows, 1), lambda pair: (0, 0)),
            block(0),
            block(pairs),
            block(2 * pairs),
            block(0),
            block(0),
            pl.BlockSpec((rows, wide), lambda pair: (0, 0)),
        ],
        out_specs=[block(0)] * 3,
        out_shape=[jax.ShapeDtypeStruct((rows, D), jnp.bfloat16)] * 3,
        compiler_params=pltpu.CompilerParams(vmem_limit_bytes=48 * 2**20),
        cost_estimate=pl.CostEstimate(
            flops=40 * rows * rows * D,
            bytes_accessed=rows * D * 16,
            transcendentals=HEADS * rows * rows,
        ),
    )(seg, qkv, qkv, qkv, mixed, grad_mixed, logs)


def bits_of(count):
    bits = count.bit_length() - 1
    assert count == 1 << bits
    return bits


def swap(value, axis, count, mask):
    return lax.ppermute(value, axis, [(i, i ^ mask) for i in range(count)])


def gather(shard, count):
    here = lax.axis_index("fsdp")
    held = shard[None]
    for bit in reversed(range(bits_of(count))):
        other = swap(held, "fsdp", count, 1 << bit)
        upper = (here >> bit) & 1 == 1
        both = jnp.where(
            upper, jnp.stack([other, held], axis=1), jnp.stack([held, other], axis=1)
        )
        held = both.reshape((-1,) + shard.shape)
    return held


def scatter(blocks, count):
    here = lax.axis_index("fsdp")
    held = blocks.astype(jnp.bfloat16)
    for bit in range(bits_of(count)):
        side = (here >> bit) & 1
        halves = held.reshape((held.shape[0] // 2, 2) + held.shape[1:])
        sent = lax.dynamic_index_in_dim(halves, 1 - side, axis=1, keepdims=False)
        kept = lax.dynamic_index_in_dim(halves, side, axis=1, keepdims=False)
        other = swap(sent, "fsdp", count, 1 << bit)
        held = (kept.astype(jnp.float32) + other.astype(jnp.float32)).astype(jnp.bfloat16)
    return held[0]


def replicas(value, count):
    for bit in range(bits_of(count)):
        other = swap(value, "rep", count, 1 << bit)
        value = (value.astype(jnp.float32) + other.astype(jnp.float32)).astype(jnp.bfloat16)
    return value


def total(value, count):
    for bit in range(bits_of(count)):
        value = value + swap(value, "fsdp", count, 1 << bit)
    return value


def adamw(weight, grad, first, second, clip, rate):
    scaled = grad * clip
    first_new = BETA_ONE * first + (1.0 - BETA_ONE) * scaled
    second_new = BETA_TWO * second + (1.0 - BETA_TWO) * scaled * scaled
    update = (
        first_new
        / (1.0 - BETA_ONE**STEP)
        / (jnp.sqrt(second_new / (1.0 - BETA_TWO**STEP)) + ADAM_EPS)
    )
    return (weight - rate * (update + DECAY * weight), first_new, second_new)


def transposed_dot(left, right):
    return jnp.einsum("ti,tj->ij", left, right, preferred_element_type=jnp.float32)


def body(
    shards_count,
    rep_count,
    pixels,
    image_tokens,
    patch_class,
    resize_coarse,
    resize_fine,
    w_base,
    w_qkv,
    w_proj,
    w_fc1,
    w_fc2,
    small_params,
    first_base,
    first_qkv,
    first_proj,
    first_fc1,
    first_fc2,
    first_small,
    second_base,
    second_qkv,
    second_proj,
    second_fc1,
    second_fc2,
    second_small,
    cotangent,
):
    bfloat = jnp.bfloat16
    rows_here = pixels.shape[0]
    here = lax.axis_index("fsdp")

    def whole(shard):
        return gather(shard.astype(bfloat), shards_count).reshape(-1, shard.shape[1])

    gathered = (
        whole(w_base),
        whole(w_qkv),
        whole(w_proj),
        whole(w_fc1),
        whole(w_fc2),
        gather(small_params.astype(bfloat), shards_count).transpose(1, 0, 2).reshape(11, D),
    )

    def resized(weights):
        coarse = jnp.dot(resize_coarse, weights[0], preferred_element_type=jnp.float32).astype(
            bfloat
        )
        finer_w = jnp.dot(resize_fine, weights[0], preferred_element_type=jnp.float32).astype(
            bfloat
        )
        return (coarse, finer_w)

    segment, alive, finer = rows_plan(image_tokens[0], patch_class[0], rows_here)
    fine_col = finer[:, None]
    coarse_weight, fine_weight = resized(gathered)
    vectors = gathered[5].astype(jnp.float32)
    patch = jnp.dot(pixels, coarse_weight, preferred_element_type=jnp.float32) * (1.0 - fine_col)
    patch = (
        patch
        + jnp.dot(pixels[:, :PIXF], fine_weight, preferred_element_type=jnp.float32) * fine_col
    )
    state_zero = patch + vectors[0]
    normed_one = layer_norm(state_zero, vectors[1], vectors[2]).astype(bfloat)
    qkv_all = jnp.dot(normed_one, gathered[1], preferred_element_type=jnp.float32).astype(bfloat)
    segment_col = segment[:, None]
    mixed, logs = attend(qkv_all, segment_col)
    state_one = (
        state_zero + jnp.dot(mixed, gathered[2], preferred_element_type=jnp.float32) + vectors[3]
    )
    normed_two = layer_norm(state_one, vectors[4], vectors[5]).astype(bfloat)
    before = jnp.dot(normed_two, gathered[3], preferred_element_type=jnp.float32) + vectors[
        7:11
    ].reshape(FF)
    hidden = gelu_exact(before).astype(bfloat)
    state_two = (
        state_one + jnp.dot(hidden, gathered[4], preferred_element_type=jnp.float32) + vectors[6]
    )
    activations = (state_two * alive[:, None]).astype(bfloat)
    grad_two = cotangent.astype(jnp.float32) * alive[:, None]
    grad_out_bias = jnp.sum(grad_two, axis=0)
    grad_branch = grad_two.astype(bfloat)
    grad_fc2 = transposed_dot(hidden, grad_branch)
    grad_hidden = jnp.dot(grad_branch, gathered[4].T, preferred_element_type=jnp.float32)
    _, gelu_back = jax.vjp(gelu_exact, before)
    grad_before = gelu_back(grad_hidden)[0].astype(bfloat)
    grad_fc1_bias = jnp.sum(grad_before.astype(jnp.float32), axis=0)
    grad_fc1 = transposed_dot(normed_two, grad_before)
    grad_normed_two = jnp.dot(grad_before, gathered[3].T, preferred_element_type=jnp.float32)
    _, norm_two_back = jax.vjp(layer_norm, state_one, vectors[4], vectors[5])
    grad_one_part, grad_gain_two, grad_shift_two = norm_two_back(grad_normed_two)
    grad_one = grad_two + grad_one_part
    grad_proj_bias = jnp.sum(grad_one, axis=0)
    grad_attn = grad_one.astype(bfloat)
    grad_proj = transposed_dot(mixed, grad_attn)
    grad_mixed = jnp.dot(grad_attn, gathered[2].T, preferred_element_type=jnp.float32).astype(
        bfloat
    )
    grad_qkv_all = jnp.concatenate(
        attend_back(qkv_all, segment_col, mixed, grad_mixed, logs), axis=1
    )
    grad_qkv = transposed_dot(normed_one, grad_qkv_all)
    grad_normed_one = jnp.dot(grad_qkv_all, gathered[1].T, preferred_element_type=jnp.float32)
    _, norm_one_back = jax.vjp(layer_norm, state_zero, vectors[1], vectors[2])
    grad_zero_part, grad_gain_one, grad_shift_one = norm_one_back(grad_normed_one)
    grad_zero = grad_one + grad_zero_part
    grad_embed_bias = jnp.sum(grad_zero, axis=0)
    grad_patch = grad_zero.astype(bfloat)
    grad_coarse_rows = grad_patch * (1.0 - fine_col).astype(bfloat)
    grad_fine_rows = grad_patch * fine_col.astype(bfloat)
    grad_coarse = transposed_dot(pixels, grad_coarse_rows)
    grad_fine = transposed_dot(pixels[:, :PIXF], grad_fine_rows)
    pixel_grad = jnp.dot(grad_coarse_rows, coarse_weight.T, preferred_element_type=jnp.float32)
    fine_pixels = jnp.dot(grad_fine_rows, fine_weight.T, preferred_element_type=jnp.float32)
    pixel_grad = (pixel_grad + jnp.pad(fine_pixels, ((0, 0), (0, PIXC - PIXF)))).astype(bfloat)
    grad_small = jnp.concatenate(
        [
            jnp.stack(
                [
                    grad_embed_bias,
                    grad_gain_one,
                    grad_shift_one,
                    grad_proj_bias,
                    grad_gain_two,
                    grad_shift_two,
                    grad_out_bias,
                ]
            ),
            grad_fc1_bias.reshape(4, D),
        ],
        axis=0,
    )
    def owned(grad, axis):
        if axis == 0:
            blocks = grad.reshape(shards_count, -1, grad.shape[1])
        else:
            blocks = grad.reshape(grad.shape[0], shards_count, -1).transpose(1, 0, 2)
        return replicas(scatter(blocks, shards_count), rep_count).astype(jnp.float32)

    pad = -(PIXC + PIXF) % (16 * shards_count)
    patch_grads = jnp.concatenate([grad_coarse, grad_fine, jnp.zeros((pad, D), jnp.float32)])
    patch_part = replicas(
        scatter(patch_grads.reshape(shards_count, -1, D), shards_count), rep_count
    )
    patch_grads = gather(patch_part, shards_count).reshape(-1, D)
    first_row = here * w_base.shape[0]
    coarse_part = lax.dynamic_slice_in_dim(resize_coarse, first_row, w_base.shape[0], axis=1)
    fine_part = lax.dynamic_slice_in_dim(resize_fine, first_row, w_base.shape[0], axis=1)
    grad_base = transposed_dot(coarse_part, patch_grads[:PIXC])
    grad_base = grad_base + transposed_dot(fine_part, patch_grads[PIXC : PIXC + PIXF])
    shards = (
        grad_base,
        owned(grad_qkv, 0),
        owned(grad_proj, 0),
        owned(grad_fc1, 0),
        owned(grad_fc2, 0),
        owned(grad_small, 1),
    )
    squares = jnp.float32(0.0)
    for shard in shards:
        squares = squares + jnp.sum(shard * shard)
    grad_norm = jnp.sqrt(total(squares, shards_count))
    clip = jnp.minimum(1.0, CLIP_NORM / grad_norm)
    masters = (w_base, w_qkv, w_proj, w_fc1, w_fc2, small_params)
    firsts = (first_base, first_qkv, first_proj, first_fc1, first_fc2, first_small)
    seconds = (second_base, second_qkv, second_proj, second_fc1, second_fc2, second_small)
    rates = (RATE, RATE, RATE, RATE, RATE, RATE_SMALL)
    results = [
        adamw(masters[index], shards[index], firsts[index], seconds[index], clip, rates[index])
        for index in range(6)
    ]
    return (
        activations,
        pixel_grad,
        grad_norm,
        results[0][0],
        results[1][0],
        results[2][0],
        results[3][0],
        results[4][0],
        results[5][0],
        results[0][1],
        results[1][1],
        results[2][1],
        results[3][1],
        results[4][1],
        results[5][1],
        results[0][2],
        results[1][2],
        results[2][2],
        results[3][2],
        results[4][2],
        results[5][2],
    )


def solution(mesh):
    in_specs = (
        P(("fsdp", "rep"), None),
        P(("fsdp", "rep"), None),
        P(("fsdp", "rep"), None),
        P(),
        P(),
        P("fsdp", None),
        P("fsdp", None),
        P("fsdp", None),
        P("fsdp", None),
        P("fsdp", None),
        P(None, "fsdp"),
        P("fsdp", None),
        P("fsdp", None),
        P("fsdp", None),
        P("fsdp", None),
        P("fsdp", None),
        P(None, "fsdp"),
        P("fsdp", None),
        P("fsdp", None),
        P("fsdp", None),
        P("fsdp", None),
        P("fsdp", None),
        P(None, "fsdp"),
        P(("fsdp", "rep"), None),
    )
    out_specs = (
        P(("fsdp", "rep"), None),
        P(("fsdp", "rep"), None),
        P(),
        P("fsdp", None),
        P("fsdp", None),
        P("fsdp", None),
        P("fsdp", None),
        P("fsdp", None),
        P(None, "fsdp"),
        P("fsdp", None),
        P("fsdp", None),
        P("fsdp", None),
        P("fsdp", None),
        P("fsdp", None),
        P(None, "fsdp"),
        P("fsdp", None),
        P("fsdp", None),
        P("fsdp", None),
        P("fsdp", None),
        P("fsdp", None),
        P(None, "fsdp"),
    )
    step = functools.partial(body, mesh.shape["fsdp"], mesh.shape["rep"])
    return jax.shard_map(step, mesh=mesh, in_specs=in_specs, out_specs=out_specs, check_vma=False)
```

time: 1150 us -> 677 us (0.59)
  waiting for transfers between devices: 487 us -> 259 us
  matrix products: 339 us -> 132 us
  starting transfers between devices: 0.5 us -> 80.1 us
  blocking collectives: 62 us -> 0 us
  Pallas kernels: 0 us -> 56.3 us
  local copies, waits for them, and re-layouts: 106 us -> 52.9 us
  other arithmetic: 122 us -> 80.1 us
    unnamed x15 -> x0, waiting for transfers between devices: 271 us -> none
    ppermute x0 -> x62, waiting for transfers between devices: none -> 259 us  [swap(): return lax.ppermute(value, axis, [(i, i ^ mask) for i in range(count)])]
    dot_general x22 -> x6, matrix products: 231 us -> 41.4 us  [the longest x1 18.6 us: body(): jnp.dot(grad_branch, gathered[4].T, preferred_element_type=jnp.float32)]
    reduce_scatter x3 -> x0, waiting for transfers between devices: 113 us -> none  [the longest x1 113 us: body(): lax.psum_scatter(grad_fc1, 'fsdp', scatter_dimension=0, tiled=True)]
    ppermute x0 -> x62, starting transfers between devices: none -> 80.1 us  [swap(): return lax.ppermute(value, axis, [(i, i ^ mask) for i in range(count)])]
    all_gather x5 -> x0, waiting for transfers between devices: 58.7 us -> none  [the longest x1 33.4 us: body(): lax.all_gather(w_qkv.astype(bfloat), 'fsdp', axis=0, tiled=True)]
    pallas_call x0 -> x2, Pallas kernels: none -> 56.3 us  [the longest x1 33.9 us: attend_back(): pl.pallas_call(functools.partial(attend_back_kernel, step=step), grid=(pa...]
    convert_element_type x10 -> x19, other arithmetic: 55.6 us -> 5.02 us  [scatter(): (kept.astype(jnp.float32) + other.astype(jnp.float32)).astype(jnp.bfloat16)]
  transfers between devices with their start and end apart: 12 -> 62, of which waited for: 8 -> 35; matrix products, arithmetic and copies ran while one was open for 40% -> 13% of each run, Pallas kernels for 0% -> 0%
where the time goes in v1:
time: 677 us; the launch traced here: 671 us
  waiting for transfers between devices  259 us (38%)
  matrix products  132 us (19%)
  other arithmetic  80.1 us (12%)
  starting transfers between devices  80.1 us (12%)
  Pallas kernels  56.3 us (8%)
  local copies, waits for them, and re-layouts  52.9 us (8%)
  between operations  10.3 us (2%)
    ppermute x62, waiting for transfers between devices, swap(): return lax.ppermute(value, axis, [(i, i ^ mask) for i in range(count)])  259 us
    ppermute x62, starting transfers between devices, swap(): return lax.ppermute(value, axis, [(i, i ^ mask) for i in range(count)])  80.1 us
    dot_general x1, matrix products, body(): jnp.dot(normed_two, gathered[3], preferred_element_type=jnp.float32)  36.1 us
    pallas_call x1, Pallas kernels, attend_back(): pl.pallas_call(functools.partial(attend_back_kernel, step=step), grid=(pa...  33.9 us
    select_n x34, other arithmetic, gather(): jnp.where(upper, jnp.stack([other, held], axis=1), jnp.stack([held, other...  33.4 us
    dot_general x8, matrix products, transposed_dot(): jnp.einsum('ti,tj->ij', left, right, preferred_element_type=jnp.float32)  31.4 us
    pallas_call x1, Pallas kernels, attend(): pl.pallas_call(functools.partial(attend_kernel, step=step), grid=(pairs,)...  22.4 us
    dot_general x1, matrix products, body(): jnp.dot(grad_branch, gathered[4].T, preferred_element_type=jnp.float32)  18.6 us
  transfers between devices with their start and end apart: 62, of which 35 were waited for; matrix products, arithmetic and copies ran while one was open for 13% of the time, Pallas kernels for 0%

profile of v1, /device:TPU:0, one launch (start us, length us, event | category | flops | bytes accessed | tf_op | source)
XLA Modules:
  0.0 670.9 jit_solution(2867164212896993890)
XLA Ops:
  23.4 19.6 %collective-permute-done.8 = bf16[1,48,2304]{2,1,0:T(8,128)(2,1)} collective-permute-done((bf16[1,48,2304]{2,1,0:T(8,128)(2,1)}, bf16[1,48,2304]{2,1,0:T(8,128)(2,1)}, u32[]{:S(2)}, u32[]{:S(2)}) %collective-permute-start.8) | collective-permute-done | bytes 221216 | tf_op jit(solution)/shard_map/ppermute | solution.py:228
  45.8 15.5 %collective-permute-done.20 = bf16[1,192,768]{2,1,0:T(8,128)(2,1)S(1)} collective-permute-done((bf16[1,192,768]{2,1,0:T(8,128)(2,1)}, bf16[1,192,768]{2,1,0:T(8,128)(2,1)S(1)}, u32[]{:S(2)}, u32[]{:S(2)}) %collective-permute-start.20) | collective-permute-done | bytes 294944 | tf_op jit(solution)/shard_map/ppermute | solution.py:228
  65.0 22.0 %collective-permute-done.21 = bf16[2,192,768]{2,1,0:T(8,128)(2,1)S(1)} collective-permute-done((bf16[2,192,768]{2,1,0:T(8,128)(2,1)S(1)}, bf16[2,192,768]{2,1,0:T(8,128)(2,1)S(1)}, u32[]{:S(2)}, u32[]{:S(2)}) %collective-permute-start.21) | collective-permute-done | bytes 589856 | tf_op jit(solution)/shard_map/ppermute | solution.py:228
  89.0 10.6 %collective-permute-done.17 = bf16[2,48,3072]{2,1,0:T(8,128)(2,1)S(1)} collective-permute-done((bf16[2,48,3072]{2,1,0:T(8,128)(2,1)S(1)}, bf16[2,48,3072]{2,1,0:T(8,128)(2,1)S(1)}, u32[]{:S(2)}, u32[]{:S(2)}) %collective-permute-start.17) | collective-permute-done | bytes 589856 | tf_op jit(solution)/shard_map/ppermute | solution.py:228
  119.7 15.5 %collective-permute-done.10 = bf16[4,48,2304]{2,1,0:T(8,128)(2,1)S(1)} collective-permute-done((bf16[4,48,2304]{2,1,0:T(8,128)(2,1)S(1)}, bf16[4,48,2304]{2,1,0:T(8,128)(2,1)S(1)}, u32[]{:S(2)}, u32[]{:S(2)}) %collective-permute-start.10) | collective-permute-done | bytes 884768 | tf_op jit(solution)/shard_map/ppermute | solution.py:228
  135.5 25.1 %collective-permute-done.18 = bf16[4,48,3072]{2,1,0:T(8,128)(2,1)S(1)} collective-permute-done((bf16[4,48,3072]{2,1,0:T(8,128)(2,1)S(1)}, bf16[4,48,3072]{2,1,0:T(8,128)(2,1)S(1)}, u32[]{:S(2)}, u32[]{:S(2)}) %collective-permute-start.18) | collective-permute-done | bytes 1179680 | tf_op jit(solution)/shard_map/ppermute | solution.py:228
  164.5 20.6 %collective-permute-done.2 = bf16[4,192,768]{2,1,0:T(8,128)(2,1)S(1)} collective-permute-done((bf16[4,192,768]{2,1,0:T(8,128)(2,1)S(1)}, bf16[4,192,768]{2,1,0:T(8,128)(2,1)S(1)}, u32[]{:S(2)}, u32[]{:S(2)}) %collective-permute-start.2) | collective-permute-done | bytes 1179680 | tf_op jit(solution)/shard_map/ppermute | solution.py:228
  217.1 6.1 maximum_select_fusion
  224.8 6.3 convolution_convert_fusion.7
  240.8 22.4 %shard_map.391 = (bf16[1024,768]{1,0:T(8,128)(2,1)S(1)}, f32[1024,128]{1,0:T(8,128)S(1)}) custom-call(s32[1024,1]{1,0:T(8,128)S(1)} %copy.169.seg_ref, bf16[1024,2304]{1,0:T(8,128)(2,1)} %convolution_convert_fusion.q_ref.k_ref.v_ref, bf16[1024,2304]{1,0:T(8,128)(2,1)} %convolution_convert_fusion.q_ref.k_ref.v_ref, ...), custom_call_target="tpu_custom_call" | custom-call | flops 12884901888 | bytes 6291456 | tf_op jit(solution)/shard_map/pallas_call | solution.py:112
  265.7 36.1 %multiply_convert_fusion = (bf16[1024,3072]{1,0:T(8,128)(2,1)}, f32[1024,3072]{1,0:T(8,128)}, f32[1024,3072]{1,0:T(8,128)}) fusion(f32[3072]{0:T(1024)S(1)} %copy-done.56, bf16[768,3072]{1,0:T(8,128)(2,1)S(1)} %bitcast.322, f32[1024,768]{0,1:T(8,128)S(1)} %get-tuple-element.200, f32[768]{0:T(1024)S(1)} %add.420, f32[768]{0:T(1024)S(1)} %mul.446, ...), kind=kOutput, calls=%fused_computation.3 | convolution fusion | flops 5043388416 | bytes 39348224 | tf_op jit(solution)/shard_map/dot_general | solution.py:357
  301.8 18.6 %fusion.115 = (bf16[3072]{0:T(1024)(128)(2,1)S(1)}, bf16[1024,3072]{1,0:T(8,128)(2,1)}) fusion(f32[1024,3072]{1,0:T(8,128)} %get-tuple-element.163, bf16[3072,768]{1,0:T(8,128)(2,1)} %bitcast.318, bf16[1024,768]{0,1:T(8,128)(2,1)} %copy.178, f32[1024]{0:T(1024)S(1)} %fusion.90, f32[1024,3072]{1,0:T(8,128)} %get-tuple-element.201, f32[3072]{0:T(1024)S(1)} %copy-done.56), kind=kOutput, calls=%fused_computation.296 | convolution fusion | flops 4884526080 | bytes 37771264 | tf_op jit(solution)/shard_map/dot_general | solution.py:369
  320.4 9.9 %fusion.114 = (bf16[768]{0:T(1024)(128)(2,1)S(1)}, f32[1024,768]{1,0:T(8,128)}) fusion(bf16[1024,3072]{1,0:T(8,128)(2,1)} %get-tuple-element.209, bf16[768,3072]{1,0:T(8,128)(2,1)} %bitcast.323), kind=kOutput, calls=%fused_computation.295 | convolution fusion | flops 4832623616 | bytes 14157312 | tf_op jit(solution)/shard_map/dot_general | solution.py:374
  330.3 7.1 %convolution_convert_fusion.2 = bf16[768,3072]{1,0:T(8,128)(2,1)} fusion(bf16[1024,3072]{1,0:T(8,128)(2,1)S(1)} %copy-done.68, f32[1024,768]{0,1:T(8,128)S(1)} %get-tuple-element.200, f32[768]{0:T(1024)S(1)} %add.420, f32[768]{0:T(1024)S(1)} %mul.446, f32[1024]{0:T(1024)S(1)} %fusion.92, f32[1024]{0:T(1024)S(1)} %broadcast_multiply_fusion), kind=kOutput, calls=%fused_computation.19 | convolution fusion | flops 4838129664 | bytes 14170112 | tf_op jit(solution)/shard_map/ti,tj->ij/dot_general | solution.py:283
  355.0 33.9 %shard_map.392 = (bf16[1024,768]{1,0:T(8,128)(2,1)S(1)}, bf16[1024,768]{1,0:T(8,128)(2,1)S(1)}, bf16[1024,768]{1,0:T(8,128)(2,1)S(1)}) custom-call(s32[1024,1]{1,0:T(8,128)S(1)} %copy.169.seg_ref, bf16[1024,2304]{1,0:T(8,128)(2,1)} %convolution_convert_fusion.q_ref.k_ref.v_ref, bf16[1024,2304]{1,0:T(8,128)(2,1)} %convolution_convert_fusion.q_ref.k_ref.v_ref, ...), custom_call_target="tpu_custom_call" | custom-call | flops 32212254720 | bytes 12582912 | tf_op jit(solution)/shard_map/pallas_call | solution.py:198
  391.0 6.2 fusion.113
  418.9 6.9 %convolution_convert_fusion.1 = bf16[3072,768]{1,0:T(8,128)(2,1)} fusion(bf16[1024,3072]{1,0:T(8,128)(2,1)S(1)} %bitcast.397, bf16[1024,768]{0,1:T(8,128)(2,1)S(1)} %copy-done.15, f32[1024]{0:T(1024)S(1)} %fusion.90), kind=kOutput, calls=%fused_computation.18 | convolution fusion | flops 4836556800 | bytes 12587008 | tf_op jit(solution)/shard_map/ti,tj->ij/dot_general | solution.py:283
  480.1 8.1 %collective-permute-done.25 = bf16[4,64,768]{2,1,0:T(8,128)(2,1)S(1)} collective-permute-done((bf16[4,64,768]{2,1,0:T(8,128)(2,1)S(1)}, bf16[4,64,768]{2,1,0:T(8,128)(2,1)S(1)}, u32[]{:S(2)}, u32[]{:S(2)}) %collective-permute-start.25) | collective-permute-done | bytes 393248 | tf_op jit(solution)/shard_map/ppermute | solution.py:228
  519.2 9.4 %collective-permute-done.31 = bf16[4,64,768]{2,1,0:T(8,128)(2,1)S(1)} collective-permute-done((bf16[4,64,768]{2,1,0:T(8,128)(2,1)S(1)}, bf16[4,64,768]{2,1,0:T(8,128)(2,1)S(1)}, u32[]{:S(2)}, u32[]{:S(2)}) %collective-permute-start.31) | collective-permute-done | bytes 393248 | tf_op jit(solution)/shard_map/ppermute | solution.py:228
  532.0 15.5 %collective-permute-done.34 = bf16[4,48,2304]{2,1,0:T(8,128)(2,1)S(1)} collective-permute-done((bf16[4,48,2304]{2,1,0:T(8,128)(2,1)S(1)}, bf16[4,48,2304]{2,1,0:T(8,128)(2,1)S(1)}, u32[]{:S(2)}, u32[]{:S(2)}) %collective-permute-start.34) | collective-permute-done | bytes 884768 | tf_op jit(solution)/shard_map/ppermute | solution.py:228
  556.3 16.5 %collective-permute-done.49 = bf16[4,192,768]{2,1,0:T(8,128)(2,1)S(1)} collective-permute-done((bf16[4,192,768]{2,1,0:T(8,128)(2,1)S(1)}, bf16[4,192,768]{2,1,0:T(8,128)(2,1)S(1)}, u32[]{:S(2)}, u32[]{:S(2)}) %collective-permute-start.49) | collective-permute-done | bytes 1179680 | tf_op jit(solution)/shard_map/ppermute | solution.py:228
  575.1 18.2 %collective-permute-done.44 = bf16[4,48,3072]{2,1,0:T(8,128)(2,1)S(1)} collective-permute-done((bf16[4,48,3072]{2,1,0:T(8,128)(2,1)S(1)}, bf16[4,48,3072]{2,1,0:T(8,128)(2,1)S(1)}, u32[]{:S(2)}, u32[]{:S(2)}) %collective-permute-start.44) | collective-permute-done | bytes 1179680 | tf_op jit(solution)/shard_map/ppermute | solution.py:228
  599.1 16.6 %collective-permute-done.45 = bf16[2,48,3072]{2,1,0:T(8,128)(2,1)S(1)} collective-permute-done((bf16[2,48,3072]{2,1,0:T(8,128)(2,1)S(1)}, bf16[2,48,3072]{2,1,0:T(8,128)(2,1)S(1)}, u32[]{:S(2)}, u32[]{:S(2)}) %collective-permute-start.45) | collective-permute-done | bytes 589856 | tf_op jit(solution)/shard_map/ppermute | solution.py:228
  619.9 10.2 %collective-permute-done.46 = bf16[1,48,3072]{2,1,0:T(8,128)(2,1)S(1)} collective-permute-done((bf16[1,48,3072]{2,1,0:T(8,128)(2,1)S(1)}, bf16[1,48,3072]{2,1,0:T(8,128)(2,1)S(1)}, u32[]{:S(2)}, u32[]{:S(2)}) %collective-permute-start.46) | collective-permute-done | bytes 294944 | tf_op jit(solution)/shard_map/ppermute | solution.py:228
  (461 shorter events, 283.6 us)
Async XLA Ops:
  7.1 94.9 %collective-permute-start.12 = (bf16[1,48,768]{2,1,0:T(8,128)(2,1)}, bf16[1,48,768]{2,1,0:T(8,128)(2,1)}, u32[]{:S(2)}, u32[]{:S(2)}) collective-permute-start(bf16[1,48,768]{2,1,0:T(8,128)(2,1)} %get-tuple-element.177), channel_id=1, source_target_pairs={{0,16},{2,18},{4,20},{6,22},{8,24},{10,26},{12,28},{14,30},{16,0},... | collective-permute-start | bytes 221192 | tf_op jit(solution)/shard_map/ppermute | solution.py:228
  8.9 34.1 %collective-permute-start.8 = (bf16[1,48,2304]{2,1,0:T(8,128)(2,1)}, bf16[1,48,2304]{2,1,0:T(8,128)(2,1)}, u32[]{:S(2)}, u32[]{:S(2)}) collective-permute-start(bf16[1,48,2304]{2,1,0:T(8,128)(2,1)} %get-tuple-element.173), channel_id=1, source_target_pairs={{0,16},{2,18},{4,20},{6,22},{8,24},{10,26},{12,28},{14,30},{16,0},... | collective-permute-start | bytes 663560 | tf_op jit(solution)/shard_map/ppermute | solution.py:228
  13.0 51.9 %collective-permute-start = (bf16[1,192,768]{2,1,0:T(8,128)(2,1)S(1)}, bf16[1,192,768]{2,1,0:T(8,128)(2,1)S(1)}, u32[]{:S(2)}, u32[]{:S(2)}) collective-permute-start(bf16[1,192,768]{2,1,0:T(8,128)(2,1)S(1)} %get-tuple-element.171), channel_id=1, source_target_pairs={{0,16},{2,18},{4,20},{6,22},{8,24},{10,26},{12,28},{14,30},{16,0},... | collective-permute-start | bytes 884744 | tf_op jit(solution)/shard_map/ppermute | solution.py:228
  14.2 48.3 %collective-permute-start.16 = (bf16[1,48,3072]{2,1,0:T(8,128)(2,1)S(1)}, bf16[1,48,3072]{2,1,0:T(8,128)(2,1)S(1)}, u32[]{:S(2)}, u32[]{:S(2)}) collective-permute-start(bf16[1,48,3072]{2,1,0:T(8,128)(2,1)S(1)} %get-tuple-element.169), channel_id=1, source_target_pairs={{0,16},{2,18},{4,20},{6,22},{8,24},{10,26},{12,28},{14,30},{16,0},... | collective-permute-start | bytes 884744 | tf_op jit(solution)/shard_map/ppermute | solution.py:228
  21.9 39.4 %collective-permute-start.20 = (bf16[1,192,768]{2,1,0:T(8,128)(2,1)}, bf16[1,192,768]{2,1,0:T(8,128)(2,1)S(1)}, u32[]{:S(2)}, u32[]{:S(2)}) collective-permute-start(bf16[1,192,768]{2,1,0:T(8,128)(2,1)} %get-tuple-element.167), channel_id=1, source_target_pairs={{0,16},{2,18},{4,20},{6,22},{8,24},{10,26},{12,28},{14,30},{16,0},... | collective-permute-start | bytes 884744 | tf_op jit(solution)/shard_map/ppermute | solution.py:228
  43.1 58.3 %collective-permute-start.5 = (bf16[2,11,48]{2,1,0:T(8,128)(2,1)S(1)}, bf16[2,11,48]{2,1,0:T(8,128)(2,1)S(1)}, u32[]{:S(2)}, u32[]{:S(2)}) collective-permute-start(bf16[2,11,48]{2,1,0:T(8,128)(2,1)S(1)} %maximum_select_fusion.32), channel_id=1, source_target_pairs={{0,8},{2,10},{4,12},{6,14},{8,0},{10,2},{12,4},{14,6},{16,24},{18,... | collective-permute-start | bytes 6344 | tf_op jit(solution)/shard_map/ppermute | solution.py:228
  64.8 34.8 %collective-permute-start.17 = (bf16[2,48,3072]{2,1,0:T(8,128)(2,1)S(1)}, bf16[2,48,3072]{2,1,0:T(8,128)(2,1)S(1)}, u32[]{:S(2)}, u32[]{:S(2)}) collective-permute-start(bf16[2,48,3072]{2,1,0:T(8,128)(2,1)S(1)} %maximum_select_fusion.17), channel_id=1, source_target_pairs={{0,8},{2,10},{4,12},{6,14},{8,0},{10,2},{12,4},{14,6},{16,24},{18,... | collective-permute-start | bytes 1769480 | tf_op jit(solution)/shard_map/ppermute | solution.py:228
  87.3 29.0 %collective-permute-start.22 = (bf16[4,192,768]{2,1,0:T(8,128)(2,1)S(1)}, bf16[4,192,768]{2,1,0:T(8,128)(2,1)S(1)}, u32[]{:S(2)}, u32[]{:S(2)}) collective-permute-start(bf16[4,192,768]{2,1,0:T(8,128)(2,1)S(1)} %bitcast.316), channel_id=1, source_target_pairs={{0,4},{2,6},{4,0},{6,2},{8,12},{10,14},{12,8},{14,10},{16,20},{18,... | collective-permute-start | bytes 3538952 | tf_op jit(solution)/shard_map/ppermute | solution.py:228
  99.7 35.6 %collective-permute-start.10 = (bf16[4,48,2304]{2,1,0:T(8,128)(2,1)S(1)}, bf16[4,48,2304]{2,1,0:T(8,128)(2,1)S(1)}, u32[]{:S(2)}, u32[]{:S(2)}) collective-permute-start(bf16[4,48,2304]{2,1,0:T(8,128)(2,1)S(1)} %bitcast.337), channel_id=1, source_target_pairs={{0,4},{2,6},{4,0},{6,2},{8,12},{10,14},{12,8},{14,10},{16,20},{18,... | collective-permute-start | bytes 2654216 | tf_op jit(solution)/shard_map/ppermute | solution.py:228
  101.3 59.2 %collective-permute-start.18 = (bf16[4,48,3072]{2,1,0:T(8,128)(2,1)S(1)}, bf16[4,48,3072]{2,1,0:T(8,128)(2,1)S(1)}, u32[]{:S(2)}, u32[]{:S(2)}) collective-permute-start(bf16[4,48,3072]{2,1,0:T(8,128)(2,1)S(1)} %bitcast.304), channel_id=1, source_target_pairs={{0,4},{2,6},{4,0},{6,2},{8,12},{10,14},{12,8},{14,10},{16,20},{18,... | collective-permute-start | bytes 3538952 | tf_op jit(solution)/shard_map/ppermute | solution.py:228
  102.0 60.9 %collective-permute-start.6 = (bf16[4,11,48]{2,0,1:T(4,128)(2,1)S(1)}, bf16[4,11,48]{2,0,1:T(4,128)(2,1)S(1)}, u32[]{:S(2)}, u32[]{:S(2)}) collective-permute-start(bf16[4,11,48]{2,0,1:T(4,128)(2,1)S(1)} %copy.163), channel_id=1, source_target_pairs={{0,4},{2,6},{4,0},{6,2},{8,12},{10,14},{12,8},{14,10},{16,20},{18,... | collective-permute-start | bytes 12680 | tf_op jit(solution)/shard_map/ppermute | solution.py:228
  110.6 51.7 %collective-permute-start.13 = (bf16[2,48,768]{2,1,0:T(8,128)(2,1)S(1)}, bf16[2,48,768]{2,1,0:T(8,128)(2,1)S(1)}, u32[]{:S(2)}, u32[]{:S(2)}) collective-permute-start(bf16[2,48,768]{2,1,0:T(8,128)(2,1)S(1)} %maximum_select_fusion.27), channel_id=1, source_target_pairs={{0,8},{2,10},{4,12},{6,14},{8,0},{10,2},{12,4},{14,6},{16,24},{18,... | collective-permute-start | bytes 442376 | tf_op jit(solution)/shard_map/ppermute | solution.py:228
  116.3 68.8 %collective-permute-start.2 = (bf16[4,192,768]{2,1,0:T(8,128)(2,1)S(1)}, bf16[4,192,768]{2,1,0:T(8,128)(2,1)S(1)}, u32[]{:S(2)}, u32[]{:S(2)}) collective-permute-start(bf16[4,192,768]{2,1,0:T(8,128)(2,1)S(1)} %bitcast.306), channel_id=1, source_target_pairs={{0,4},{2,6},{4,0},{6,2},{8,12},{10,14},{12,8},{14,10},{16,20},{18,... | collective-permute-start | bytes 3538952 | tf_op jit(solution)/shard_map/ppermute | solution.py:228
  135.3 68.6 %collective-permute-start.23 = (bf16[8,192,768]{2,1,0:T(8,128)(2,1)}, bf16[8,192,768]{2,1,0:T(8,128)(2,1)}, u32[]{:S(2)}, u32[]{:S(2)}) collective-permute-start(bf16[8,192,768]{2,1,0:T(8,128)(2,1)} %bitcast.70), channel_id=1, source_target_pairs={{0,2},{2,0},{4,6},{6,4},{8,10},{10,8},{12,14},{14,12},{16,18},{18,... | collective-permute-start | bytes 7077896 | tf_op jit(solution)/shard_map/ppermute | solution.py:228
  160.5 40.4 %collective-permute-start.11 = (bf16[8,48,2304]{2,1,0:T(8,128)(2,1)S(1)}, bf16[8,48,2304]{2,1,0:T(8,128)(2,1)}, u32[]{:S(2)}, u32[]{:S(2)}) collective-permute-start(bf16[8,48,2304]{2,1,0:T(8,128)(2,1)S(1)} %bitcast.298), channel_id=1, source_target_pairs={{0,2},{2,0},{4,6},{6,4},{8,10},{10,8},{12,14},{14,12},{16,18},{18,... | collective-permute-start | bytes 5308424 | tf_op jit(solution)/shard_map/ppermute | solution.py:228
  162.3 49.8 %collective-permute-start.19 = (bf16[8,48,3072]{2,1,0:T(8,128)(2,1)}, bf16[8,48,3072]{2,1,0:T(8,128)(2,1)}, u32[]{:S(2)}, u32[]{:S(2)}) collective-permute-start(bf16[8,48,3072]{2,1,0:T(8,128)(2,1)} %bitcast.59), channel_id=1, source_target_pairs={{0,2},{2,0},{4,6},{6,4},{8,10},{10,8},{12,14},{14,12},{16,18},{18,... | collective-permute-start | bytes 7077896 | tf_op jit(solution)/shard_map/ppermute | solution.py:228
  188.3 28.8 %collective-permute-start.3 = (bf16[8,192,768]{2,1,0:T(8,128)(2,1)}, bf16[8,192,768]{2,1,0:T(8,128)(2,1)}, u32[]{:S(2)}, u32[]{:S(2)}) collective-permute-start(bf16[8,192,768]{2,1,0:T(8,128)(2,1)} %bitcast.8), channel_id=1, source_target_pairs={{0,2},{2,0},{4,6},{6,4},{8,10},{10,8},{12,14},{14,12},{16,18},{18,... | collective-permute-start | bytes 7077896 | tf_op jit(solution)/shard_map/ppermute | solution.py:228
  437.2 91.6 %collective-permute-start.48 = (bf16[8,192,768]{2,1,0:T(8,128)(2,1)}, bf16[8,192,768]{2,1,0:T(8,128)(2,1)S(1)}, u32[]{:S(2)}, u32[]{:S(2)}) collective-permute-start(bf16[8,192,768]{2,1,0:T(8,128)(2,1)} %dynamic-slice_bitcast_fusion), channel_id=1, source_target_pairs={{0,2},{2,0},{4,6},{6,4},{8,10},{10,8},{12,14},{14,12},{16,18},{18,... | collective-permute-start | bytes 7077896 | tf_op jit(solution)/shard_map/ppermute | solution.py:228
  441.8 36.4 %collective-permute-start.38 = (bf16[8,48,768]{2,1,0:T(8,128)(2,1)}, bf16[8,48,768]{2,1,0:T(8,128)(2,1)}, u32[]{:S(2)}, u32[]{:S(2)}) collective-permute-start(bf16[8,48,768]{2,1,0:T(8,128)(2,1)} %dynamic-slice_bitcast_fusion.9), channel_id=1, source_target_pairs={{0,2},{2,0},{4,6},{6,4},{8,10},{10,8},{12,14},{14,12},{16,18},{18,... | collective-permute-start | bytes 1769480 | tf_op jit(solution)/shard_map/ppermute | solution.py:228
  459.2 71.9 %collective-permute-start.43 = (bf16[8,48,3072]{2,1,0:T(8,128)(2,1)S(1)}, bf16[8,48,3072]{2,1,0:T(8,128)(2,1)S(1)}, u32[]{:S(2)}, u32[]{:S(2)}) collective-permute-start(bf16[8,48,3072]{2,1,0:T(8,128)(2,1)S(1)} %dynamic-slice_bitcast_fusion.1), channel_id=1, source_target_pairs={{0,2},{2,0},{4,6},{6,4},{8,10},{10,8},{12,14},{14,12},{16,18},{18,... | collective-permute-start | bytes 7077896 | tf_op jit(solution)/shard_map/ppermute | solution.py:228
  472.4 45.7 %collective-permute-start.33 = (bf16[8,48,2304]{2,1,0:T(8,128)(2,1)S(1)}, bf16[8,48,2304]{2,1,0:T(8,128)(2,1)S(1)}, u32[]{:S(2)}, u32[]{:S(2)}) collective-permute-start(bf16[8,48,2304]{2,1,0:T(8,128)(2,1)S(1)} %dynamic-slice_bitcast_fusion.2), channel_id=1, source_target_pairs={{0,2},{2,0},{4,6},{6,4},{8,10},{10,8},{12,14},{14,12},{16,18},{18,... | collective-permute-start | bytes 5308424 | tf_op jit(solution)/shard_map/ppermute | solution.py:228
  518.6 28.9 %collective-permute-start.34 = (bf16[4,48,2304]{2,1,0:T(8,128)(2,1)S(1)}, bf16[4,48,2304]{2,1,0:T(8,128)(2,1)S(1)}, u32[]{:S(2)}, u32[]{:S(2)}) collective-permute-start(bf16[4,48,2304]{2,1,0:T(8,128)(2,1)S(1)} %dynamic-slice_bitcast_fusion.5), channel_id=1, source_target_pairs={{0,4},{2,6},{4,0},{6,2},{8,12},{10,14},{12,8},{14,10},{16,20},{18,... | collective-permute-start | bytes 2654216 | tf_op jit(solution)/shard_map/ppermute | solution.py:228
  529.5 43.4 %collective-permute-start.49 = (bf16[4,192,768]{2,1,0:T(8,128)(2,1)S(1)}, bf16[4,192,768]{2,1,0:T(8,128)(2,1)S(1)}, u32[]{:S(2)}, u32[]{:S(2)}) collective-permute-start(bf16[4,192,768]{2,1,0:T(8,128)(2,1)S(1)} %dynamic-slice_bitcast_fusion.3), channel_id=1, source_target_pairs={{0,4},{2,6},{4,0},{6,2},{8,12},{10,14},{12,8},{14,10},{16,20},{18,... | collective-permute-start | bytes 3538952 | tf_op jit(solution)/shard_map/ppermute | solution.py:228
  549.9 43.4 %collective-permute-start.44 = (bf16[4,48,3072]{2,1,0:T(8,128)(2,1)S(1)}, bf16[4,48,3072]{2,1,0:T(8,128)(2,1)S(1)}, u32[]{:S(2)}, u32[]{:S(2)}) collective-permute-start(bf16[4,48,3072]{2,1,0:T(8,128)(2,1)S(1)} %dynamic-slice_bitcast_fusion.4), channel_id=1, source_target_pairs={{0,4},{2,6},{4,0},{6,2},{8,12},{10,14},{12,8},{14,10},{16,20},{18,... | collective-permute-start | bytes 3538952 | tf_op jit(solution)/shard_map/ppermute | solution.py:228
  (115 other events, 1537.9 us)

commit v2 on v1

v2 whole, which is shorter than its diff:
```python
import functools
import math

import jax
import jax.numpy as jnp
from jax import lax
from jax.experimental import pallas as pl
from jax.experimental.pallas import tpu as pltpu
from jax.sharding import PartitionSpec as P

D = 768
HEADS = 12
HEAD_DIM = 64
FF = 3072
PIXC = 768
PIXF = 192
PIXALL = 1024
STEP = 10
SLOTS = 5
SMALL = 11
SMALL_PAD = 16


EPS_NORM = 1e-06
RATE = 0.05
RATE_SMALL = 0.5
BETA_ONE = 0.9
BETA_TWO = 0.95
ADAM_EPS = 1e-08
DECAY = 0.05
CLIP_NORM = 1.0

LOG2E = math.log2(math.e)
FAR = -1e30
ATT_ROWS = 512
ROWS = 256
VMEM = 24 * 2**20
BF = jnp.bfloat16
F32 = jnp.float32
ANY = pl.ANY


def rows_plan(lengths, classes, count):
    ends = jnp.cumsum(lengths)
    positions = jnp.arange(count, dtype=jnp.int32)
    segment = jnp.sum((positions[:, None] >= ends[None, :]).astype(jnp.int32), axis=1)
    alive = (positions < ends[-1]).astype(F32)
    slots = jnp.arange(lengths.shape[0], dtype=jnp.int32)
    member = (segment[:, None] == slots[None, :]).astype(F32)
    finer = jnp.sum(member * classes[None, :].astype(F32), axis=1)
    return (segment, alive, finer)


def adamw(weight, grad, first, second, clip, rate):
    scaled = grad * clip
    first_new = BETA_ONE * first + (1.0 - BETA_ONE) * scaled
    second_new = BETA_TWO * second + (1.0 - BETA_TWO) * scaled * scaled
    update = (
        first_new
        / (1.0 - BETA_ONE**STEP)
        / (jnp.sqrt(second_new / (1.0 - BETA_TWO**STEP)) + ADAM_EPS)
    )
    return (weight - rate * (update + DECAY * weight), first_new, second_new)


def dot_nn(left, right):
    return jnp.dot(left, right, preferred_element_type=F32)


def dot_nt(left, right):
    return lax.dot_general(left, right, (((1,), (1,)), ((), ())), preferred_element_type=F32)


def dot_tn(left, right):
    return lax.dot_general(left, right, (((0,), (0,)), ((), ())), preferred_element_type=F32)


def norm_parts(values):
    average = jnp.mean(values, axis=-1, keepdims=True)
    centre = values - average
    spread = jnp.mean(centre * centre, axis=-1, keepdims=True)
    scale = lax.rsqrt(spread + EPS_NORM)
    return centre * scale, scale


def norm_back(grad, gain, unit, scale):
    inner = grad * gain
    mean_inner = jnp.mean(inner, axis=-1, keepdims=True)
    mean_unit = jnp.mean(inner * unit, axis=-1, keepdims=True)
    return scale * (inner - mean_inner - unit * mean_unit)


def column_sum(values):
    return jnp.sum(values, axis=0, keepdims=True)


def fetch(ids_ref, refs, offsets, target, sems, column=0, width=None):
    me = ids_ref[0]
    copies = []
    for ref, places in zip(refs, offsets):
        rows = ref.shape[1]
        for index, place in enumerate(places):
            source = ref.at[index]
            if width is not None and width != ref.shape[2]:
                source = ref.at[index, :, pl.ds(column, width)]
            first = 0 if place is None else jnp.bitwise_xor(me, place) * rows
            if place is not None:
                first = pl.multiple_of(first, rows)
            copies.append(
                pltpu.make_async_copy(
                    source, target.at[pl.ds(first, rows)], sems.at[len(copies)]
                )
            )
    return copies


def begin(copies):
    for copy in copies:
        copy.start()


def finish(copies):
    for copy in copies:
        copy.wait()


def piece_count(weight):
    return sum(len(places) for places in weight[1])


def anys(count):
    return [pl.BlockSpec(memory_space=ANY)] * count


def params(**others):
    return pltpu.CompilerParams(vmem_limit_bytes=VMEM, **others)


def cost():
    return pl.CostEstimate(flops=0, bytes_accessed=0, transcendentals=0)


def skip(kernel, count):
    if count == 0:
        return kernel
    return lambda ids_ref, *refs: kernel(ids_ref, *refs[count:])


def tie(value, *others):
    return lax.optimization_barrier((value,) + others)[0]


def row_spec(width, step=ROWS):
    return pl.BlockSpec((step, width), lambda i, ids: (i, 0))


def full_spec(shape):
    return pl.BlockSpec(shape, lambda i, ids: (0,) * len(shape))


def resize_kernel(ids_ref, *refs, offsets, arrays, shard_rows):
    coarse_ref, fine_ref = refs[:2]
    pieces = refs[2 : 2 + arrays]
    out_ref, resize, base, small, sems = refs[2 + arrays :]
    me = ids_ref[0]
    core = jnp.bitwise_and(me, 1)
    side = jnp.bitwise_and(lax.shift_right_logical(me, 1), 1)
    half = PIXALL // 2
    width = 2 * shard_rows
    blocks = resize.shape[1] // width
    rest = PIXC - half

    def spans(low):
        copies = []
        for block in range(blocks):
            source = pl.ds(pl.multiple_of((2 * block + side) * width, 128), width)
            target = pl.ds(block * width, width)
            at = 2 * block
            if low:
                copies.append(
                    pltpu.make_async_copy(
                        coarse_ref.at[pl.ds(0, half), source],
                        resize.at[pl.ds(0, half), target],
                        sems.at[at],
                    )
                )
            else:
                copies.append(
                    pltpu.make_async_copy(
                        coarse_ref.at[pl.ds(half, rest), source],
                        resize.at[pl.ds(0, rest), target],
                        sems.at[at],
                    )
                )
                copies.append(
                    pltpu.make_async_copy(
                        fine_ref.at[:, source],
                        resize.at[pl.ds(rest, PIXF), target],
                        sems.at[at + 1],
                    )
                )
        return copies

    copies = []
    at = 2 * blocks
    small_at = 0
    for ref, places in zip(pieces, offsets):
        for index, place in enumerate(places):
            shard = jnp.bitwise_xor(me, place)
            spot = lax.shift_right_logical(shard, 2) * 2 + jnp.bitwise_and(shard, 1)
            first = pl.multiple_of(spot * shard_rows, shard_rows)
            copies.append(
                pltpu.make_async_copy(
                    ref.at[index, pl.ds(0, shard_rows)],
                    base.at[pl.ds(first, shard_rows)],
                    sems.at[at],
                )
            )
            copies.append(
                pltpu.make_async_copy(
                    ref.at[index, pl.ds(shard_rows, 2 * SMALL_PAD)],
                    small.at[small_at],
                    sems.at[at + 1],
                )
            )
            at += 2
            small_at += 1
    begin(copies)

    @pl.when(core == 0)
    def _():
        low = spans(True)
        begin(low)
        finish(low)

    @pl.when(core != 0)
    def _():
        resize[pl.ds(rest + PIXF, half - rest - PIXF)] = jnp.zeros(
            (half - rest - PIXF, resize.shape[1]), BF
        )
        high = spans(False)
        begin(high)
        finish(high)

    finish(copies)
    out_ref[:half] = dot_nn(resize[...], base[...]).astype(BF)
    joined = small[0].astype(F32)
    for index in range(1, small_at):
        joined = joined + small[index].astype(F32)
    out_ref[half:] = joined.astype(BF)


def resize_part(ids, coarse, fine, arrays, offsets, shard_rows):
    half = PIXALL // 2
    count = sum(len(places) for places in offsets)
    blocks = count // 2
    return pl.pallas_call(
        functools.partial(
            resize_kernel, offsets=offsets, arrays=len(arrays), shard_rows=shard_rows
        ),
        grid_spec=pltpu.PrefetchScalarGridSpec(
            num_scalar_prefetch=1,
            grid=(1,),
            in_specs=anys(2 + len(arrays)),
            out_specs=full_spec((half + 2 * SMALL_PAD, D // 2)),
            scratch_shapes=[
                pltpu.VMEM((half, count * shard_rows), BF),
                pltpu.VMEM((count * shard_rows, D // 2), BF),
                pltpu.VMEM((count, 2 * SMALL_PAD, D // 2), BF),
                pltpu.SemaphoreType.DMA((2 * blocks + 2 * count,)),
            ],
        ),
        out_shape=jax.ShapeDtypeStruct((half + 2 * SMALL_PAD, D // 2), BF),
        compiler_params=params(),
        cost_estimate=cost(),
        name="resize_part",
    )(ids, coarse, fine, *arrays)


def spread_pixels(pixels, fine_col):
    rough = jnp.where(fine_col > 0.5, jnp.zeros((), BF), pixels)
    wide = PIXALL - PIXC
    lane = lax.broadcasted_iota(jnp.int32, (pixels.shape[0], wide), 1)
    fine = jnp.where((lane < PIXF) & (fine_col > 0.5), pixels[:, :wide], jnp.zeros((), BF))
    return jnp.concatenate([rough, fine], axis=1)


def patch_kernel(ids_ref, pixels_ref, rows_ref, vectors_ref, *refs, places, arrays):
    pieces = refs[:arrays]
    state_ref, normed_ref, weight_ref, sems = refs[arrays:]

    @pl.when(pl.program_id(0) == 0)
    def _():
        copies = []
        for ref, spots in zip(pieces, places):
            for index, spot in enumerate(spots):
                rows, width = ref.shape[1:]
                first, column = (0, 0) if spot is None else spot
                if spot is not None:
                    first = jnp.bitwise_xor(jnp.bitwise_and(ids_ref[0], 1), first) * rows
                    column = jnp.bitwise_xor(ids_ref[1], column) * width
                    first = pl.multiple_of(first, rows)
                    column = pl.multiple_of(column, 128)
                copies.append(
                    pltpu.make_async_copy(
                        ref.at[index],
                        weight_ref.at[pl.ds(first, rows), pl.ds(column, width)],
                        sems.at[len(copies)],
                    )
                )
        begin(copies)
        finish(copies)

    pixels = spread_pixels(pixels_ref[...], rows_ref[:, 2:3])
    vectors = vectors_ref[...]
    state = dot_nn(pixels, weight_ref[...]) + vectors[0:1]
    unit, _ = norm_parts(state)
    state_ref[...] = state
    normed_ref[...] = (unit * vectors[1:2] + vectors[2:3]).astype(BF)


def patch(ids, pixels, rows, vectors, arrays, places, deps=()):
    count = pixels.shape[0]
    total = sum(len(spots) for spots in places)
    return pl.pallas_call(
        skip(functools.partial(patch_kernel, places=places, arrays=len(arrays)), len(deps)),
        grid_spec=pltpu.PrefetchScalarGridSpec(
            num_scalar_prefetch=1,
            grid=(count // ROWS,),
            in_specs=anys(len(deps)) + [row_spec(PIXC), row_spec(8), full_spec(vectors.shape)]
            + anys(len(arrays)),
            out_specs=[row_spec(D), row_spec(D), full_spec((PIXALL, D))],
            scratch_shapes=[pltpu.SemaphoreType.DMA((total,))],
        ),
        out_shape=[
            jax.ShapeDtypeStruct((count, D), F32),
            jax.ShapeDtypeStruct((count, D), BF),
            jax.ShapeDtypeStruct((PIXALL, D), BF),
        ],
        compiler_params=params(),
        cost_estimate=cost(),
        name="patch",
    )(ids, *deps, pixels, rows, vectors, *arrays)


def qkv_kernel(ids_ref, normed_ref, *refs, offsets, arrays):
    pieces = refs[:arrays]
    out_ref, weight, sems = refs[arrays:]

    @pl.when(pl.program_id(0) == 0)
    def _():
        copies = fetch(ids_ref, pieces, offsets, weight, sems)
        begin(copies)
        finish(copies)

    out_ref[...] = dot_nn(normed_ref[...], weight[...]).astype(BF)


def project_qkv(ids, normed, weight, deps=()):
    arrays, offsets = weight
    count = normed.shape[0]
    return pl.pallas_call(
        skip(functools.partial(qkv_kernel, offsets=offsets, arrays=len(arrays)), len(deps)),
        grid_spec=pltpu.PrefetchScalarGridSpec(
            num_scalar_prefetch=1,
            grid=(count // ROWS,),
            in_specs=anys(len(deps)) + [row_spec(D)] + anys(len(arrays)),
            out_specs=row_spec(3 * D),
            scratch_shapes=[
                pltpu.VMEM((D, 3 * D), BF),
                pltpu.SemaphoreType.DMA((piece_count(weight),)),
            ],
        ),
        out_shape=jax.ShapeDtypeStruct((count, 3 * D), BF),
        compiler_params=params(),
        cost_estimate=cost(),
        name="project_qkv",
    )(ids, *deps, normed, *arrays)


def lane_plan(rows, side, seg):
    lane = lax.broadcasted_iota(jnp.int32, (rows, 2 * HEAD_DIM), 1)
    mine = (lane < HEAD_DIM) if side == 0 else (lane >= HEAD_DIM)
    first = HEAD_DIM if side == 0 else 0
    hot = lane - first == seg
    slots = (lane >= first) & (lane < first + SLOTS)
    return lane, mine, hot, slots


def attend_kernel(ids_ref, seg_ref, q_ref, k_ref, v_ref, mixed_ref, log_ref, *, step, start):
    pair = pl.program_id(0) + start
    rows = q_ref.shape[0]
    seg = seg_ref[...]
    one = jnp.ones((), BF)
    logs = jnp.where(pair == start, 0.0, log_ref[...])
    outs = []
    for side in range(2):
        lane, mine, hot, slots = lane_plan(rows, side, seg)
        keys = jnp.where(
            mine, k_ref[...], jnp.where(slots & ~hot, FAR, 0.0).astype(BF)
        )
        values = jnp.where(mine, v_ref[...], one)
        queries = jnp.where(mine, q_ref[...] * BF(0.125), hot.astype(BF))
        parts, part_logs = [], []
        for at in range(0, rows, step):
            scores = lax.dot_general(
                queries[at : at + step],
                keys,
                (((1,), (1,)), ((), ())),
                preferred_element_type=F32,
            )
            top = jnp.max(scores, axis=1, keepdims=True) * LOG2E
            raised = jnp.exp2(scores * LOG2E - top).astype(BF)
            sums = jnp.dot(raised, values, preferred_element_type=F32)
            turned = pltpu.roll(sums, HEAD_DIM, 1)
            inside = mine[at : at + step]
            parts.append(sums / turned)
            part_logs.append(top + jnp.log2(jnp.where(inside, turned, sums)))
        outs.append(jnp.concatenate(parts, axis=0))
        logs = jnp.where(lane == 2 * pair + side, jnp.concatenate(part_logs, axis=0), logs)
    lane = lax.broadcasted_iota(jnp.int32, (rows, 2 * HEAD_DIM), 1)
    mixed_ref[...] = jnp.where(lane < HEAD_DIM, outs[0], outs[1]).astype(BF)
    log_ref[...] = logs


def attend(ids, qkv, seg, start, many, deps=()):
    rows = qkv.shape[0]
    wide = 2 * HEAD_DIM
    pairs = D // wide
    step = min(ATT_ROWS, rows)

    def block(first):
        return pl.BlockSpec((rows, wide), lambda pair, ids: (0, first + start + pair))

    return pl.pallas_call(
        skip(functools.partial(attend_kernel, step=step, start=start), len(deps)),
        grid_spec=pltpu.PrefetchScalarGridSpec(
            num_scalar_prefetch=1,
            grid=(many,),
            in_specs=anys(len(deps))
            + [full_spec((rows, 1)), block(0), block(pairs), block(2 * pairs)],
            out_specs=[
                pl.BlockSpec((rows, wide), lambda pair, ids: (0, pair)),
                full_spec((rows, wide)),
            ],
        ),
        out_shape=[
            jax.ShapeDtypeStruct((rows, many * wide), BF),
            jax.ShapeDtypeStruct((rows, wide), F32),
        ],
        compiler_params=params(),
        cost_estimate=cost(),
        name="attend",
    )(ids, *deps, seg, qkv, qkv, qkv)


def attend_back_kernel(
    ids_ref, seg_ref, q_ref, k_ref, v_ref, mixed_ref, grad_ref, log_ref, out_ref, *, step, start
):
    pair = pl.program_id(0) + start
    rows = q_ref.shape[0]
    seg = seg_ref[...]
    zero = jnp.zeros((), BF)
    product = grad_ref[...].astype(F32) * mixed_ref[...].astype(F32)
    plain_keys = k_ref[...]
    values = v_ref[...]
    scaled = q_ref[...] * BF(0.125)
    results = []
    for side in range(2):
        lane, mine, hot, slots = lane_plan(rows, side, seg)
        keys = jnp.where(
            mine, plain_keys, jnp.where(slots & ~hot, FAR, 0.0).astype(BF)
        )
        queries = jnp.where(mine, scaled, hot.astype(BF))
        grads = jnp.where(mine, grad_ref[...], zero)
        queries_t = jnp.where(mine, scaled, zero).T
        grads_t = grads.T
        drop = jnp.sum(jnp.where(mine, product, 0.0), axis=1, keepdims=True)
        logs = jnp.sum(
            jnp.where(lane == 2 * pair + side, log_ref[...], 0.0), axis=1, keepdims=True
        )
        dq_parts, dk_t, dv_t = [], 0.0, 0.0
        for at in range(0, rows, step):
            part = slice(at, at + step)
            scores = lax.dot_general(
                queries[part],
                keys,
                (((1,), (1,)), ((), ())),
                preferred_element_type=F32,
            )
            probs = jnp.exp2(scores * LOG2E - logs[part])
            grad_probs = lax.dot_general(
                grads[part],
                values,
                (((1,), (1,)), ((), ())),
                preferred_element_type=F32,
            )
            grad_scores = (probs * (grad_probs - drop[part])).astype(BF)
            probs = probs.astype(BF)
            dq_parts.append(jnp.dot(grad_scores, plain_keys, preferred_element_type=F32))
            dv_t = dv_t + jnp.dot(grads_t[:, part], probs, preferred_element_type=F32)
            dk_t = dk_t + jnp.dot(
                queries_t[:, part], grad_scores, preferred_element_type=F32
            )
        results.append((jnp.concatenate(dq_parts, axis=0) * 0.125, dk_t.T, dv_t.T))
    lane = lax.broadcasted_iota(jnp.int32, (rows, 2 * HEAD_DIM), 1)
    for kind, (low, high) in enumerate(zip(results[0], results[1])):
        out_ref[kind] = jnp.where(lane < HEAD_DIM, low, high).astype(BF)


def attend_back(ids, qkv, seg, mixed, grad_mixed, logs, start, many, deps=()):
    rows = qkv.shape[0]
    wide = 2 * HEAD_DIM
    pairs = D // wide
    step = min(ATT_ROWS, rows)

    def block(first):
        return pl.BlockSpec((rows, wide), lambda pair, ids: (0, first + start + pair))

    kernel = functools.partial(attend_back_kernel, step=step, start=start)
    return pl.pallas_call(
        skip(kernel, len(deps)),
        grid_spec=pltpu.PrefetchScalarGridSpec(
            num_scalar_prefetch=1,
            grid=(many,),
            in_specs=anys(len(deps))
            + [
                full_spec((rows, 1)),
                block(0),
                block(pairs),
                block(2 * pairs),
                block(0),
                block(0),
                full_spec((rows, wide)),
            ],
            out_specs=pl.BlockSpec((3, rows, wide), lambda pair, ids: (0, 0, pair)),
        ),
        out_shape=jax.ShapeDtypeStruct((3, rows, many * wide), BF),
        compiler_params=params(),
        cost_estimate=cost(),
        name="attend_back",
    )(ids, *deps, seg, qkv, qkv, qkv, mixed, grad_mixed, logs)


def up_kernel(
    ids_ref, mixed_ref, state_ref, vectors_ref, bias_ref, *refs, offsets, arrays, columns
):
    pieces = refs[:arrays]
    one_ref, normed_ref, hidden_ref, slope_ref, proj, up, proj_sems, up_sems = refs[arrays:]

    @pl.when(pl.program_id(0) == 0)
    def _():
        copies = fetch(ids_ref, pieces, offsets, proj, proj_sems, 0, D)
        copies = copies + fetch(ids_ref, pieces, offsets, up, up_sems, D, FF)
        begin(copies)
        finish(copies)

    vectors = vectors_ref[...]
    state = state_ref[...] + dot_nn(mixed_ref[...], proj[...]) + vectors[3:4]
    one_ref[...] = state
    unit, _ = norm_parts(state)
    normed = (unit * vectors[4:5] + vectors[5:6]).astype(BF)
    normed_ref[...] = normed
    for at in range(0, FF, columns):
        part = slice(at, at + columns)
        before = dot_nn(normed, up[:, part]) + bias_ref[:, part]
        share = 0.5 + 0.5 * lax.erf(before * math.sqrt(0.5))
        bell = jnp.exp2(before * before * (-0.5 * LOG2E)) * (1.0 / math.sqrt(2.0 * math.pi))
        hidden_ref[:, part] = (before * share).astype(BF)
        slope_ref[:, part] = (share + before * bell).astype(BF)


def feed_up(ids, mixed, state, vectors, bias, weight, deps=()):
    arrays, offsets = weight
    count = mixed.shape[0]
    total = piece_count(weight)
    return pl.pallas_call(
        skip(functools.partial(up_kernel, offsets=offsets, arrays=len(arrays), columns=512), len(deps)),
        grid_spec=pltpu.PrefetchScalarGridSpec(
            num_scalar_prefetch=1,
            grid=(count // ROWS,),
            in_specs=anys(len(deps)) + [
                row_spec(D),
                row_spec(D),
                full_spec(vectors.shape),
                full_spec(bias.shape),
            ]
            + anys(len(arrays)),
            out_specs=[row_spec(D), row_spec(D), row_spec(FF), row_spec(FF)],
            scratch_shapes=[
                pltpu.VMEM((D, D), BF),
                pltpu.VMEM((D, FF), BF),
                pltpu.SemaphoreType.DMA((total,)),
                pltpu.SemaphoreType.DMA((total,)),
            ],
        ),
        out_shape=[
            jax.ShapeDtypeStruct((count, D), F32),
            jax.ShapeDtypeStruct((count, D), BF),
            jax.ShapeDtypeStruct((count, FF), BF),
            jax.ShapeDtypeStruct((count, FF), BF),
        ],
        compiler_params=params(),
        cost_estimate=cost(),
        name="feed_up",
    )(ids, *deps, mixed, state, vectors, bias, *arrays)


def down_kernel(
    ids_ref,
    hidden_ref,
    slope_ref,
    state_ref,
    cotangent_ref,
    rows_ref,
    vectors_ref,
    *refs,
    offsets,
    arrays,
    columns,
):
    pieces = refs[:arrays]
    out_ref, branch_ref, before_ref, sums_ref, weight, sems = refs[arrays:]

    @pl.when(pl.program_id(0) == 0)
    def _():
        copies = fetch(ids_ref, pieces, offsets, weight, sems)
        begin(copies)
        sums_ref[...] = jnp.zeros_like(sums_ref)
        finish(copies)

    alive = rows_ref[:, 1:2]
    state = state_ref[...] + dot_nn(hidden_ref[...], weight[...]) + vectors_ref[6:7]
    out_ref[...] = (state * alive).astype(BF)
    grad = cotangent_ref[...].astype(F32) * alive
    branch = grad.astype(BF)
    branch_ref[...] = branch
    sums_ref[0:1, :D] += column_sum(grad)
    for at in range(0, FF, columns):
        part = slice(at, at + columns)
        before = dot_nt(branch, weight[part]) * slope_ref[:, part].astype(F32)
        before = before.astype(BF)
        before_ref[:, part] = before
        sums_ref[1:2, part] += column_sum(before.astype(F32))


def feed_down(ids, hidden, slope, state, cotangent, rows, vectors, weight, deps=()):
    arrays, offsets = weight
    count = hidden.shape[0]
    return pl.pallas_call(
        skip(functools.partial(down_kernel, offsets=offsets, arrays=len(arrays), columns=768), len(deps)),
        grid_spec=pltpu.PrefetchScalarGridSpec(
            num_scalar_prefetch=1,
            grid=(count // ROWS,),
            in_specs=anys(len(deps)) + [
                row_spec(FF),
                row_spec(FF),
                row_spec(D),
                row_spec(D),
                row_spec(8),
                full_spec(vectors.shape),
            ]
            + anys(len(arrays)),
            out_specs=[row_spec(D), row_spec(D), row_spec(FF), full_spec((8, FF))],
            scratch_shapes=[
                pltpu.VMEM((FF, D), BF),
                pltpu.SemaphoreType.DMA((piece_count(weight),)),
            ],
        ),
        out_shape=[
            jax.ShapeDtypeStruct((count, D), BF),
            jax.ShapeDtypeStruct((count, D), BF),
            jax.ShapeDtypeStruct((count, FF), BF),
            jax.ShapeDtypeStruct((8, FF), F32),
        ],
        compiler_params=params(),
        cost_estimate=cost(),
        name="feed_down",
    )(ids, *deps, hidden, slope, state, cotangent, rows, vectors, *arrays)


def middle_kernel(
    ids_ref, before_ref, state_ref, branch_ref, vectors_ref, *refs, offsets, arrays
):
    pieces = refs[:arrays]
    grad_ref, attn_ref, mixed_ref, sums_ref, proj, up, proj_sems, up_sems = refs[arrays:]

    @pl.when(pl.program_id(0) == 0)
    def _():
        copies = fetch(ids_ref, pieces, offsets, proj, proj_sems, 0, D)
        copies = copies + fetch(ids_ref, pieces, offsets, up, up_sems, D, FF)
        begin(copies)
        sums_ref[...] = jnp.zeros_like(sums_ref)
        finish(copies)

    vectors = vectors_ref[...]
    normed = dot_nt(before_ref[...], up[...])
    unit, scale = norm_parts(state_ref[...])
    grad = branch_ref[...].astype(F32) + norm_back(normed, vectors[4:5], unit, scale)
    grad_ref[...] = grad
    attn = grad.astype(BF)
    attn_ref[...] = attn
    mixed_ref[...] = dot_nt(attn, proj[...]).astype(BF)
    sums_ref[0:1] += column_sum(grad)
    sums_ref[1:2] += column_sum(normed * unit)
    sums_ref[2:3] += column_sum(normed)


def middle_back(ids, before, state, branch, vectors, weight, deps=()):
    arrays, offsets = weight
    count = before.shape[0]
    total = piece_count(weight)
    return pl.pallas_call(
        skip(functools.partial(middle_kernel, offsets=offsets, arrays=len(arrays)), len(deps)),
        grid_spec=pltpu.PrefetchScalarGridSpec(
            num_scalar_prefetch=1,
            grid=(count // ROWS,),
            in_specs=anys(len(deps)) + [row_spec(FF), row_spec(D), row_spec(D), full_spec(vectors.shape)]
            + anys(len(arrays)),
            out_specs=[row_spec(D), row_spec(D), row_spec(D), full_spec((8, D))],
            scratch_shapes=[
                pltpu.VMEM((D, D), BF),
                pltpu.VMEM((D, FF), BF),
                pltpu.SemaphoreType.DMA((total,)),
                pltpu.SemaphoreType.DMA((total,)),
            ],
        ),
        out_shape=[
            jax.ShapeDtypeStruct((count, D), F32),
            jax.ShapeDtypeStruct((count, D), BF),
            jax.ShapeDtypeStruct((count, D), BF),
            jax.ShapeDtypeStruct((8, D), F32),
        ],
        compiler_params=params(),
        cost_estimate=cost(),
        name="middle_back",
    )(ids, *deps, before, state, branch, vectors, *arrays)


def place_pieces(ids_ref, values, kept_ref, sent_ref, shards, rows, first, lead=0):
    count = values.shape[0] // rows
    flat = len(kept_ref.shape) == 2
    if sent_ref is None:
        if flat:
            kept_ref[lead:] = values
        else:
            kept_ref[pl.ds(first, count)] = values.reshape((count, rows) + values.shape[1:])
        return
    me = ids_ref[0]
    for index in range(count):
        apart = jnp.bitwise_xor(me, first + index)
        spot = 0
        for bit in range(1, bits_of(shards)):
            spot = spot * 2 + jnp.bitwise_and(lax.shift_right_logical(apart, bit), 1)
        piece = values[index * rows : (index + 1) * rows]
        same = jnp.bitwise_and(apart, 1) == 0

        def put(ref, piece=piece, spot=spot):
            if flat:
                ref[pl.ds(pl.multiple_of(lead + spot * rows, 16), rows)] = piece
            else:
                ref[spot] = piece

        pl.when(same)(functools.partial(put, kept_ref))
        pl.when(jnp.logical_not(same))(functools.partial(put, sent_ref))


def weight_kernel(ids_ref, left_ref, right_ref, *refs, shards, rows, first_step, extra):
    out_refs = refs[2 * extra :]
    sent_ref = out_refs[1] if len(out_refs) > 1 else None
    step = pl.program_id(0)

    def put(left_ref, right_ref):
        right = right_ref[0] if len(right_ref.shape) == 3 else right_ref[...]
        values = dot_tn(left_ref[...], right).astype(BF)
        place_pieces(
            ids_ref, values, out_refs[0], sent_ref, shards, rows, step * first_step
        )

    if extra:
        last = pl.num_programs(0) - extra * (refs[1].shape[1] // right_ref.shape[2])
        pl.when(step < last)(lambda: put(left_ref, right_ref))

        @pl.when(step >= last)
        def _():
            wide = right_ref.shape[2]
            for index in range(refs[1].shape[1] // wide):
                part = pl.ds(index * wide, wide)

                @pl.when(step == last + index)
                def _(part=part):
                    put(refs[0], refs[1].at[:, part])

    else:
        put(left_ref, right_ref)


def weight_grad(ids, left, right, shards, split, name, deps=(), extra=()):
    count, tall = left.shape
    stacked = right.ndim == 3
    wide = right.shape[-1]
    step = wide if stacked else min(768, max(tall, wide))
    narrow = tall > wide and not stacked
    rows = tall // shards
    outs = 2 if split else 1
    pieces = shards // outs
    more_specs = []
    if narrow:
        grid, first_step, out_wide = tall // step, step // rows, wide
        specs = [
            pl.BlockSpec((count, step), lambda i, ids: (0, i)),
            pl.BlockSpec((count, wide), lambda i, ids: (0, 0)),
        ]
        out_spec = pl.BlockSpec((pieces, rows, wide), lambda i, ids: (0, 0, 0))
    else:
        first_step = 0
        if stacked:
            kinds = right.shape[0]
            grid, out_wide = kinds, kinds * wide
            if extra:
                grid, out_wide = grid + extra[1].shape[1] // wide, out_wide + extra[1].shape[1]
                more_specs = [full_spec(value.shape) for value in extra]
            right_spec = pl.BlockSpec(
                (1, count, step), lambda i, ids: (jnp.minimum(i, kinds - 1), 0, 0)
            )
        else:
            grid, out_wide = wide // step, wide
            right_spec = pl.BlockSpec((count, step), lambda i, ids: (0, i))
        specs = [pl.BlockSpec((count, tall), lambda i, ids: (0, 0)), right_spec]
        out_spec = pl.BlockSpec((pieces, rows, step), lambda i, ids: (0, 0, i))
    kernel = functools.partial(
        weight_kernel,
        shards=shards,
        rows=rows,
        first_step=first_step,
        extra=1 if extra else 0,
    )
    return pl.pallas_call(
        skip(kernel, len(deps)),
        grid_spec=pltpu.PrefetchScalarGridSpec(
            num_scalar_prefetch=1,
            grid=(grid,),
            in_specs=anys(len(deps)) + specs + more_specs,
            out_specs=[out_spec] * outs,
        ),
        out_shape=[jax.ShapeDtypeStruct((pieces, rows, out_wide), BF)] * outs,
        compiler_params=params(),
        cost_estimate=cost(),
        name=name,
    )(ids, *deps, left, right, *extra)


def embed_kernel(
    ids_ref,
    state_ref,
    grad_ref,
    vectors_ref,
    down_sums_ref,
    middle_sums_ref,
    *refs,
    offsets,
    arrays,
    chunks,
):
    grad_refs = refs[:chunks]
    pieces = refs[chunks : chunks + arrays]
    patch_ref, small_ref, weight, sums, sems = refs[chunks + arrays :]
    step = pl.program_id(0)

    @pl.when(step == 0)
    def _():
        copies = fetch(ids_ref, pieces, offsets, weight, sems)
        begin(copies)
        sums[...] = jnp.zeros_like(sums)
        finish(copies)

    normed = 0.0
    at = 0
    for ref in grad_refs:
        wide = ref.shape[2]
        for kind in range(3):
            first = kind * D + at
            normed = normed + dot_nt(ref[kind], weight[:, first : first + wide])
        at += wide
    unit, scale = norm_parts(state_ref[...])
    grad = grad_ref[...] + norm_back(normed, vectors_ref[1:2], unit, scale)
    patch_ref[...] = grad.astype(BF)
    sums[0:1] += column_sum(grad)
    sums[1:2] += column_sum(normed * unit)
    sums[2:3] += column_sum(normed)

    @pl.when(step == pl.num_programs(0) - 1)
    def _():
        small = [sums[0:3], middle_sums_ref[0:3], down_sums_ref[0:1, :D]]
        small += [
            down_sums_ref[1:2, index * D : (index + 1) * D] for index in range(FF // D)
        ]
        small += [jnp.zeros((SMALL_PAD - SMALL, D), F32)]
        small_ref[:, :D] = jnp.concatenate(small, axis=0).astype(BF)
        small_ref[:, D:] = jnp.zeros((SMALL_PAD, PIXALL - D), BF)


def embed_back(
    ids, grads, state, grad, vectors, down_sums, middle_sums, weight, deps=()
):
    arrays, offsets = weight
    count = state.shape[0]
    kernel = functools.partial(
        embed_kernel, offsets=offsets, arrays=len(arrays), chunks=len(grads)
    )
    return pl.pallas_call(
        skip(kernel, len(deps)),
        grid_spec=pltpu.PrefetchScalarGridSpec(
            num_scalar_prefetch=1,
            grid=(count // ROWS,),
            in_specs=anys(len(deps))
            + [
                row_spec(D),
                row_spec(D),
                full_spec(vectors.shape),
                full_spec(down_sums.shape),
                full_spec(middle_sums.shape),
            ]
            + [
                pl.BlockSpec((3, ROWS, part.shape[2]), lambda i, ids: (0, i, 0))
                for part in grads
            ]
            + anys(len(arrays)),
            out_specs=[row_spec(D), full_spec((SMALL_PAD, PIXALL))],
            scratch_shapes=[
                pltpu.VMEM((D, 3 * D), BF),
                pltpu.VMEM((8, D), F32),
                pltpu.SemaphoreType.DMA((piece_count(weight),)),
            ],
        ),
        out_shape=[
            jax.ShapeDtypeStruct((count, D), BF),
            jax.ShapeDtypeStruct((SMALL_PAD, PIXALL), BF),
        ],
        compiler_params=params(),
        cost_estimate=cost(),
        name="embed_back",
    )(ids, *deps, state, grad, vectors, down_sums, middle_sums, *grads, *arrays)


def patch_back_kernel(ids_ref, patch_ref, pixels_ref, rows_ref, small_ref, *out_refs, shards):
    sent_ref = out_refs[1] if len(out_refs) > 1 else None
    spread = spread_pixels(pixels_ref[...], rows_ref[:, 2:3])
    values = dot_tn(patch_ref[...], spread).astype(BF)
    place_pieces(
        ids_ref, values, out_refs[0], sent_ref, shards, D // shards, 0, SMALL_PAD
    )
    for ref in out_refs:
        ref[:SMALL_PAD] = small_ref[...]


def patch_back(ids, patch_grad, pixels, rows, small, shards, split, deps=()):
    count = pixels.shape[0]
    outs = 2 if split else 1
    held = (SMALL_PAD + D // outs, PIXALL)
    return pl.pallas_call(
        skip(functools.partial(patch_back_kernel, shards=shards), len(deps)),
        grid_spec=pltpu.PrefetchScalarGridSpec(
            num_scalar_prefetch=1,
            grid=(1,),
            in_specs=anys(len(deps))
            + [
                full_spec((count, D)),
                full_spec((count, PIXC)),
                full_spec(rows.shape),
                full_spec(small.shape),
            ],
            out_specs=[full_spec(held)] * outs,
        ),
        out_shape=[jax.ShapeDtypeStruct(held, BF)] * outs,
        compiler_params=params(),
        cost_estimate=cost(),
        name="patch_back",
    )(ids, *deps, patch_grad, pixels, rows, small)


def pixel_kernel(ids_ref, patch_ref, rows_ref, weight_ref, out_ref):
    fine = rows_ref[:, 2:3]
    both = dot_nt(patch_ref[...], weight_ref[...])
    wide = PIXALL - PIXC
    rough = both[:, :PIXC] * (1.0 - fine)
    first = rough[:, :wide] + both[:, PIXC:] * fine
    out_ref[...] = jnp.concatenate([first, rough[:, wide:]], axis=1).astype(BF)


def pixel_back(ids, patch_grad, rows, weight, deps=()):
    count = patch_grad.shape[0]
    return pl.pallas_call(
        skip(pixel_kernel, len(deps)),
        grid_spec=pltpu.PrefetchScalarGridSpec(
            num_scalar_prefetch=1,
            grid=(count // ROWS,),
            in_specs=anys(len(deps)) + [row_spec(D), row_spec(8), full_spec(weight.shape)],
            out_specs=row_spec(PIXC),
        ),
        out_shape=jax.ShapeDtypeStruct((count, PIXC), BF),
        compiler_params=params(),
        cost_estimate=cost(),
        name="pixel_back",
    )(ids, *deps, patch_grad, rows, weight)


def bits_of(count):
    bits = count.bit_length() - 1
    assert count == 1 << bits
    return bits


def swap(value, axis, count, mask):
    return lax.ppermute(value, axis, [(i, i ^ mask) for i in range(count)])


def add_low(left, right):
    return (left.astype(F32) + right.astype(F32)).astype(BF)


class Gather:
    def __init__(self, shard, count):
        self.held, self.places, self.count = shard[None], [0], count
        self.bits = list(reversed(range(2, bits_of(count))))
        self.other = None

    def land(self, *after):
        if self.other is not None:
            self.held = jnp.concatenate([self.held, tie(self.other, *after)])
            self.other = None
        return self.held

    def step(self, *after):
        bit = self.bits.pop(0)
        held = tie(self.land(*after), *after)
        self.other = swap(held, "fsdp", self.count, 1 << bit)
        self.places = self.places + [place ^ (1 << bit) for place in self.places]
        return self.other

    def far(self, *after):
        held = tie(self.land(*after), *after)
        self.other = swap(held, "fsdp", self.count, 2)
        self.held_core = swap(held, "fsdp", self.count, 1)
        return self.other

    def near(self, *after):
        other_core = swap(tie(self.other, *after), "fsdp", self.count, 1)
        offsets = tuple(tuple(p ^ mask for p in self.places) for mask in (0, 1, 2, 3))
        return (self.held, self.held_core, self.other, other_core), offsets


def gather_whole(shard, count):
    here = lax.axis_index("fsdp")
    held = shard[None]
    for bit in reversed(range(bits_of(count))):
        other = swap(held, "fsdp", count, 1 << bit)
        upper = (here >> bit) & 1 == 1
        both = jnp.where(
            upper, jnp.stack([other, held], axis=1), jnp.stack([held, other], axis=1)
        )
        held = both.reshape((-1,) + shard.shape)
    return held.reshape((-1,) + shard.shape[1:])


def as_piece(whole):
    return (whole[None],), ((None,),)


def scatter_whole(blocks, count):
    here = lax.axis_index("fsdp")
    held = blocks
    for bit in range(bits_of(count)):
        side = (here >> bit) & 1
        halves = held.reshape((held.shape[0] // 2, 2) + held.shape[1:])
        sent = lax.dynamic_index_in_dim(halves, 1 - side, axis=1, keepdims=False)
        kept = lax.dynamic_index_in_dim(halves, side, axis=1, keepdims=False)
        held = add_low(kept, swap(sent, "fsdp", count, 1 << bit))
    return held[0]


class Scatter:
    def __init__(self, parts, shards, reps, lead=0, early=False):
        self.kept, self.sent = parts
        self.shards, self.reps, self.lead = shards, reps, lead
        bits = list(range(1, bits_of(shards)))
        self.plan = [0] + (["half"] + bits + ["join"] if early else bits + ["rep"])
        self.at = 0
        self.ready = self.sent

    def step(self, *after):
        kind = self.plan[self.at]
        value = tie(self.ready, *after)
        if isinstance(kind, int):
            self.other = swap(value, "fsdp", self.shards, 1 << kind)
        else:
            self.other = swap(value, "rep", self.reps, 1)
        self.at += 1

    def land(self, *after):
        kept, other = self.kept, tie(self.other, *after)
        following = self.plan[self.at] if self.at < len(self.plan) else None
        there = lax.axis_index("rep")
        if self.plan[self.at - 1] == "join":
            low = jnp.where(there == 0, kept, other)
            high = jnp.where(there == 0, other, kept)
            self.kept = self.ready = jnp.concatenate([low, high], axis=-1)
        elif following == "half":
            wide = kept.shape[-1] // 2

            def columns(side):
                return add_low(
                    lax.dynamic_slice_in_dim(kept, side * wide, wide, axis=2),
                    lax.dynamic_slice_in_dim(other, side * wide, wide, axis=2),
                )

            self.kept, self.ready = columns(there), columns(1 - there)
        elif isinstance(following, int):
            half = (kept.shape[0] - self.lead) // 2 + self.lead
            low, high = add_low(kept[:half], other[:half]), add_low(kept[half:], other[half:])
            self.kept, self.ready = low, high
            if self.lead:
                self.ready = jnp.concatenate([low[: self.lead], high])
        else:
            self.kept = self.ready = add_low(kept, other)
        return self.ready


def replicas(value, count):
    for bit in range(bits_of(count)):
        value = add_low(value, swap(value, "rep", count, 1 << bit))
    return value


def total_of(value, count):
    for bit in range(bits_of(count)):
        value = value + swap(value, "fsdp", count, 1 << bit)
    return value


def body(
    shards,
    reps,
    pixels,
    image_tokens,
    patch_class,
    resize_coarse,
    resize_fine,
    w_base,
    w_qkv,
    w_proj,
    w_fc1,
    w_fc2,
    small_params,
    first_base,
    first_qkv,
    first_proj,
    first_fc1,
    first_fc2,
    first_small,
    second_base,
    second_qkv,
    second_proj,
    second_fc1,
    second_fc2,
    second_small,
    cotangent,
):
    rows_here = pixels.shape[0]
    here = lax.axis_index("fsdp")
    there = lax.axis_index("rep")
    ids = jnp.stack([here, there]).astype(jnp.int32)
    base_rows = w_base.shape[0]
    pieced = shards == 16 and reps == 2 and w_qkv.shape[0] % 16 == 0

    segment, alive, finer = rows_plan(image_tokens[0], patch_class[0], rows_here)
    segment_col = segment[:, None]
    nothing = jnp.zeros_like(alive)
    rows = jnp.stack([nothing, alive, finer] + [nothing] * 5, axis=1)

    low_qkv = w_qkv.astype(BF)
    low_both = jnp.concatenate([w_proj, w_fc1], axis=1).astype(BF)
    low_fc2 = w_fc2.astype(BF)
    small_cols = small_params.shape[1]
    if pieced:
        half_cols = D // 2
        lanes = jnp.arange(D, dtype=jnp.int32)[None, :] // small_cols
        placed = jnp.where(lanes == here, jnp.tile(small_params, (1, shards)), 0.0)
        placed = jnp.pad(placed, ((0, SMALL_PAD - SMALL), (0, 0))).astype(BF)
        mine = lax.dynamic_slice_in_dim(w_base, there * half_cols, half_cols, axis=1)
        message = jnp.concatenate(
            [mine.astype(BF), placed[:, :half_cols], placed[:, half_cols:]], axis=0
        )
        gather_base = Gather(message, shards)
        gather_base.step()
        base_done = gather_base.step()
        held, places = gather_base.land(), gather_base.places
        other = swap(held, "fsdp", shards, 1)
        offsets = (tuple(places), tuple(place ^ 1 for place in places))
        part = resize_part(ids, resize_coarse, resize_fine, (held, other), offsets, base_rows)
        gather_qkv = Gather(low_qkv, shards)
        gather_qkv.step(base_done)
        qkv_done = gather_qkv.step(part)
        part = add_low(part, swap(part, "fsdp", shards, 2))
        half_rows = PIXALL // 2
        quarter = part[:half_rows][None]
        small_low = part[half_rows:]
        vectors = jnp.concatenate([small_low[:SMALL_PAD], small_low[SMALL_PAD:]], axis=1)
        quarter_rep = swap(quarter, "rep", reps, 1)
        quarter_core = swap(quarter, "fsdp", shards, 1)
        quarter_both = swap(quarter_rep, "fsdp", shards, 1)
        patch_arrays = (quarter, quarter_core, quarter_rep, quarter_both)
        patch_places = (((0, 0),), ((1, 0),), ((0, 1),), ((1, 1),))
        gather_qkv.far(quarter)
        gather_both = Gather(low_both, shards)
        gather_both.step(qkv_done, quarter)
    else:
        base = gather_whole(w_base.astype(BF), shards)
        coarse = dot_nn(resize_coarse, base).astype(BF)
        fine = dot_nn(resize_fine, base).astype(BF)
        whole = jnp.concatenate([coarse, fine, jnp.zeros((PIXALL - PIXC - PIXF, D), BF)])
        patch_arrays = (whole[None],)
        patch_places = ((None,),)
        vectors = gather_whole(small_params.astype(BF).T, shards).T
        vectors = jnp.pad(vectors, ((0, SMALL_PAD - SMALL), (0, 0)))
        weight_qkv = as_piece(gather_whole(low_qkv, shards))
        weight_both = as_piece(gather_whole(low_both, shards))
        weight_fc2 = as_piece(gather_whole(low_fc2, shards))
    vectors = vectors.astype(F32)
    bias = vectors[7:11].reshape(1, FF)

    state_zero, normed_one, patch_weight = patch(
        ids, pixels, rows, vectors, patch_arrays, patch_places
    )
    if pieced:
        weight_qkv = gather_qkv.near(state_zero)
        both_done = gather_both.step(state_zero)
    qkv = project_qkv(ids, normed_one, weight_qkv)
    front = attend(ids, qkv, segment_col, 0, HEADS // 4)
    after = ()
    if pieced:
        both_held = gather_both.land(front[0])
        both_far = gather_both.far(front[0])
        gather_fc2 = Gather(low_fc2, shards)
        fc2_done = gather_fc2.step(front[0], both_done)
        after = (both_held,)
    back = attend(ids, qkv, segment_col, HEADS // 4, HEADS // 4, after)
    if pieced:
        fc2_done = gather_fc2.step(back[0])
        weight_both = gather_both.near(fc2_done)
        fc2_far = gather_fc2.far(both_far)
    mixed = jnp.concatenate([front[0], back[0]], axis=1)
    logs = front[1] + back[1]
    state_one, normed_two, hidden, slope = feed_up(
        ids, mixed, state_zero, vectors, bias, weight_both
    )
    if pieced:
        weight_fc2 = gather_fc2.near(state_one)
    activations, branch, grad_before, down_sums = feed_down(
        ids, hidden, slope, state_one, cotangent, rows, vectors, weight_fc2
    )

    chunks = 3
    pairs = HEADS // 2

    def qkv_chunk(index, *after):
        many = pairs // chunks
        return attend_back(
            ids, qkv, segment_col, mixed, grad_mixed, logs, index * many, many, after
        )

    def chunk_grad(part, *after, extra=()):
        return weight_grad(
            ids, normed_one, part, shards, pieced, "grad_qkv", after, extra
        )

    def finish_embed(grads, *after):
        return embed_back(
            ids,
            grads,
            state_zero,
            grad_one,
            vectors,
            down_sums,
            middle_sums,
            weight_qkv,
            after,
        )

    part_fc2 = weight_grad(ids, hidden, branch, shards, pieced, "grad_fc2")
    if pieced:
        sum_fc2 = Scatter(part_fc2, shards, reps)
        sum_fc2.step()
        part_fc1 = weight_grad(
            ids, normed_two, grad_before, shards, pieced, "grad_fc1", part_fc2
        )
        sum_fc1 = Scatter(part_fc1, shards, reps, early=True)
        sum_fc2.land(part_fc1[0])
        sum_fc2.step()
        sum_fc1.step()
        grad_one, grad_attn, grad_mixed, middle_sums = middle_back(
            ids,
            grad_before,
            state_one,
            branch,
            vectors,
            weight_both,
            (sum_fc2.ready, part_fc1[0]),
        )
        sum_fc1.land(grad_one)
        sum_fc1.step()
        first = qkv_chunk(0, sum_fc1.ready)
        part_first = chunk_grad(first, extra=(mixed, grad_attn))
        sum_first = Scatter(part_first, shards, reps, early=True)
        sum_fc2.land(part_first[0])
        sum_fc2.step()
        sum_first.step()
        second = qkv_chunk(1, sum_fc2.ready, part_first[0])
        sum_first.land(second)
        sum_first.step()
        sum_fc1.land(second)
        sum_fc1.step()
        part_second = chunk_grad(second, sum_first.ready, sum_fc1.ready)
        sum_second = Scatter(part_second, shards, reps)
        sum_fc2.land(part_second[0])
        sum_fc2.step()
        sum_second.step()
        third = qkv_chunk(2, sum_fc2.ready, part_second[0])
        sum_second.land(third)
        sum_first.land(third)
        sum_first.step()
        sum_second.step(sum_first.ready)
        part_third = chunk_grad(third, sum_first.ready, sum_second.ready)
        sum_third = Scatter(part_third, shards, reps)
        sum_third.step()
        sum_fc1.land(part_third[0])
        sum_fc1.step()
        patch_grad, small_part = finish_embed(
            (first, second, third), part_third[0], sum_fc1.ready
        )
        sum_third.land(patch_grad)
        sum_third.step()
        sum_first.land(patch_grad)
        sum_first.step()
        sum_fc2.land(patch_grad)
        sum_fc2.step()
        patch_parts = patch_back(
            ids,
            patch_grad,
            pixels,
            rows,
            small_part,
            shards,
            pieced,
            (sum_third.ready, sum_first.ready, sum_fc2.ready),
        )
        sum_patch = Scatter(patch_parts, shards, reps, SMALL_PAD)
        sum_patch.step()
        sum_second.land(patch_parts[0])
        sum_second.step()
        sum_fc1.land(patch_parts[0])
        sum_fc1.step()
        sum_patch.land()
        sum_patch.step(sum_second.ready, sum_fc1.ready)
        pixel_grad = pixel_back(ids, patch_grad, rows, patch_weight, (sum_patch.ready,))
        sum_third.land(pixel_grad)
        sum_third.step()
        sum_first.land(pixel_grad)
        sum_first.step()
        sum_fc2.land(pixel_grad)
        sum_patch.land(sum_third.ready, sum_first.ready)
        sum_patch.step()
        mark = sum_patch.ready
        sum_second.land(mark)
        sum_second.step()
        sum_fc1.land(mark)
        sum_fc1.step()
        sum_third.land(mark)
        sum_third.step()
        sum_first.land(mark)
        sum_first.step()
        sum_patch.land(sum_second.ready, sum_fc1.ready, sum_third.ready)
        sum_patch.step()
        mark = sum_patch.ready
        sum_second.land(mark)
        sum_second.step()
        sum_third.land(mark)
        sum_third.step()
        sum_fc1.land(mark)
        sum_first.land(mark)
        sum_patch.land(sum_second.ready, sum_third.ready)
        sum_patch.step()
        mark = sum_patch.ready
        sum_second.land(mark)
        sum_third.land(mark)
        sum_patch.land()
        grad_fc2, grad_fc1 = sum_fc2.ready[0], sum_fc1.ready[0]
        grad_first, grad_proj = sum_first.ready[0, :, :D], sum_first.ready[0, :, D:]
        grad_second, grad_third = sum_second.ready[0], sum_third.ready[0]
        turned = sum_patch.ready
    else:

        def owned(parts):
            return replicas(scatter_whole(parts[0], shards), reps)

        grad_fc2 = owned(part_fc2)
        grad_fc1 = owned(
            weight_grad(ids, normed_two, grad_before, shards, pieced, "grad_fc1")
        )
        grad_one, grad_attn, grad_mixed, middle_sums = middle_back(
            ids, grad_before, state_one, branch, vectors, weight_both
        )
        grad_proj = owned(weight_grad(ids, mixed, grad_attn, shards, pieced, "grad_proj"))
        grads = [qkv_chunk(index) for index in range(chunks)]
        grad_first, grad_second, grad_third = [owned(chunk_grad(part)) for part in grads]
        patch_grad, small_part = finish_embed(grads)
        patch_parts = patch_back(ids, patch_grad, pixels, rows, small_part, shards, pieced)
        pixel_grad = pixel_back(ids, patch_grad, rows, patch_weight)
        small_all = small_part
        for bit in range(bits_of(shards)):
            small_all = add_low(small_all, swap(small_all, "fsdp", shards, 1 << bit))
        patch_all = patch_parts[0][SMALL_PAD:].reshape(shards, D // shards, PIXALL)
        turned = jnp.concatenate([replicas(small_all, reps), owned((patch_all,))])

    small_total = turned[:SMALL, :D].astype(F32)
    turned = turned[SMALL_PAD:]
    grad_small = lax.dynamic_slice_in_dim(small_total, here * small_cols, small_cols, axis=1)
    resize = jnp.concatenate(
        [resize_coarse, resize_fine, jnp.zeros((PIXALL - PIXC - PIXF, resize_fine.shape[1]), BF)]
    )
    base_cols = dot_nn(turned, resize)
    squares = jnp.sum(base_cols * base_cols)
    pieces = base_cols.astype(BF).reshape(base_cols.shape[0], shards, base_rows)
    pieces = lax.all_to_all(pieces.transpose(1, 0, 2), "fsdp", 0, 0)
    grad_base = pieces.reshape(D, base_rows).T
    wide = grad_first.shape[1] // 3
    grad_qkv = jnp.concatenate(
        [
            part[:, kind * wide : (kind + 1) * wide]
            for kind in range(3)
            for part in (grad_first, grad_second, grad_third)
        ],
        axis=1,
    )

    shards_of = [
        value.astype(F32) for value in (grad_base, grad_qkv, grad_proj, grad_fc1, grad_fc2)
    ] + [grad_small]
    for shard in shards_of[1:5]:
        squares = squares + jnp.sum(shard * shard)
    squares = total_of(squares, shards) + jnp.sum(small_total * small_total)
    grad_norm = jnp.sqrt(squares)
    clip = jnp.minimum(1.0, CLIP_NORM / grad_norm)
    masters = (w_base, w_qkv, w_proj, w_fc1, w_fc2, small_params)
    firsts = (first_base, first_qkv, first_proj, first_fc1, first_fc2, first_small)
    seconds = (second_base, second_qkv, second_proj, second_fc1, second_fc2, second_small)
    rates = (RATE, RATE, RATE, RATE, RATE, RATE_SMALL)
    results = [
        adamw(masters[index], shards_of[index], firsts[index], seconds[index], clip, rates[index])
        for index in range(6)
    ]
    return (activations, pixel_grad, grad_norm) + tuple(
        results[index][kind] for kind in range(3) for index in range(6)
    )


def solution(mesh):
    tokens = P(("fsdp", "rep"), None)
    split_rows = P("fsdp", None)
    states = (split_rows,) * 5 + (P(None, "fsdp"),)
    in_specs = (tokens, tokens, tokens, P(), P()) + states * 3 + (tokens,)
    out_specs = (tokens, tokens, P()) + states * 3
    step = functools.partial(body, mesh.shape["fsdp"], mesh.shape["rep"])
    return jax.shard_map(
        step, mesh=mesh, in_specs=in_specs, out_specs=out_specs, check_vma=False
    )
```

time: 677 us -> 422 us (0.62)
  waiting for transfers between devices: 259 us -> 84.9 us
  matrix products: 132 us -> 2.09 us
  Pallas kernels: 56.3 us -> 163 us
  other arithmetic: 80.1 us -> 45.6 us
  local copies, waits for them, and re-layouts: 52.9 us -> 40 us
  starting transfers between devices: 80.1 us -> 72.3 us
    ppermute x62 -> x58, waiting for transfers between devices: 259 us -> 84.9 us  [swap(): return lax.ppermute(value, axis, [(i, i ^ mask) for i in range(count)])]
    dot_general x22 -> x1, matrix products: 132 us -> 2.09 us  [dot_nn(): return jnp.dot(left, right, preferred_element_type=F32)]
    pallas_call x2 -> x19, Pallas kernels: 56.3 us -> 163 us  [the longest x3 35.5 us: attend_back(): pl.pallas_call(skip(kernel, len(deps)), grid_spec=pltpu.PrefetchScalarGri...]
    select_n x34 -> x1, other arithmetic: 33.4 us -> 0.03 us  [land(): low = jnp.where(there == 0, kept, other)]
    convert_element_type x22 -> x33, other arithmetic: 6.28 us -> 25.8 us  [the longest x30 25.1 us: add_low(): return (left.astype(F32) + right.astype(F32)).astype(BF)]
    unnamed x169 -> x213, local copies, waits for them, and re-layouts: 17.1 us -> 34.4 us
    reduce_sum x9 -> x2, other arithmetic: 15.4 us -> 0.69 us  [the longest x1 0.61 us: body(): squares = total_of(squares, shards) + jnp.sum(small_total * small_total)]
    ppermute x62 -> x58, starting transfers between devices: 80.1 us -> 68.5 us  [swap(): return lax.ppermute(value, axis, [(i, i ^ mask) for i in range(count)])]
  transfers between devices with their start and end apart: 62 -> 59, of which waited for: 35 -> 22; matrix products, arithmetic and copies ran while one was open for 13% -> 11% of each run, Pallas kernels for 0% -> 34%
where the time goes in v2:
time: 422 us; the launch traced here: 418 us
  Pallas kernels  163 us (39%)
  waiting for transfers between devices  84.9 us (20%)
  starting transfers between devices  72.3 us (17%)
  other arithmetic  45.6 us (11%)
  local copies, waits for them, and re-layouts  40 us (9%)
  between operations  10.4 us (2%)
    ppermute x58, waiting for transfers between devices, swap(): return lax.ppermute(value, axis, [(i, i ^ mask) for i in range(count)])  84.9 us
    ppermute x58, starting transfers between devices, swap(): return lax.ppermute(value, axis, [(i, i ^ mask) for i in range(count)])  68.5 us
    pallas_call x3, Pallas kernels, attend_back(): pl.pallas_call(skip(kernel, len(deps)), grid_spec=pltpu.PrefetchScalarGri...  35.5 us
    unnamed x213, local copies, waits for them, and re-layouts  34.4 us
    pallas_call x5, Pallas kernels, weight_grad(): pl.pallas_call(skip(kernel, len(deps)), grid_spec=pltpu.PrefetchScalarGri...  30.6 us
    convert_element_type x30, other arithmetic, add_low(): return (left.astype(F32) + right.astype(F32)).astype(BF)  25.1 us
    pallas_call x2, Pallas kernels, attend(): pl.pallas_call(skip(functools.partial(attend_kernel, step=step, start=sta...  23.1 us
    pallas_call x1, Pallas kernels, feed_up(): pl.pallas_call(skip(functools.partial(up_kernel, offsets=offsets, arrays=...  14 us
  transfers between devices with their start and end apart: 59, of which 22 were waited for; matrix products, arithmetic and copies ran while one was open for 11% of the time, Pallas kernels for 34%

profile of v2, /device:TPU:0, one launch (start us, length us, event | category | flops | bytes accessed | tf_op | source)
XLA Modules:
  0.0 417.7 jit_solution(12810205737375888130)
XLA Ops:
  7.8 7.0 %collective-permute-done = bf16[1,224,384]{2,1,0:T(8,128)(2,1)S(1)} collective-permute-done((bf16[1,224,384]{2,1,0:T(8,128)(2,1)S(1)}, bf16[1,224,384]{2,1,0:T(8,128)(2,1)S(1)}, u32[]{:S(2)}, u32[]{:S(2)}) %collective-permute-start) | collective-permute-done | bytes 172064 | tf_op jit(solution)/shard_map/ppermute | solution.py:1015
  16.5 7.6 %collective-permute-done.1 = bf16[2,224,384]{2,1,0:T(8,128)(2,1)S(1)} collective-permute-done((bf16[2,224,384]{2,1,0:T(8,128)(2,1)S(1)}, bf16[2,224,384]{2,1,0:T(8,128)(2,1)S(1)}, u32[]{:S(2)}, u32[]{:S(2)}) %collective-permute-start.1) | collective-permute-done | bytes 344096 | tf_op jit(solution)/shard_map/ppermute | solution.py:1015
  39.2 6.4 %collective-permute-done.3 = bf16[544,384]{1,0:T(8,128)(2,1)S(1)} collective-permute-done((bf16[544,384]{1,0:T(8,128)(2,1)S(1)}, bf16[544,384]{1,0:T(8,128)(2,1)S(1)}, u32[]{:S(2)}, u32[]{:S(2)}) %collective-permute-start.3) | collective-permute-done | bytes 417824 | tf_op jit(solution)/shard_map/ppermute | solution.py:1015
  64.5 4.3 %patch.1 = (f32[1024,768]{1,0:T(8,128)S(1)}, bf16[1024,768]{1,0:T(8,128)(2,1)S(1)}, bf16[1024,768]{1,0:T(8,128)(2,1)S(1)}) custom-call(s32[2]{0:T(128)S(1)} %pad_add_fusion.ids_ref, bf16[1024,768]{1,0:T(8,128)(2,1)S(1)} %copy-done.29, f32[1024,8]{1,0:T(8,128)S(1)} %copy.65.rows_ref.refs_5_.refs_2_, ...), custom_call_target="tpu_custom_call" | custom-call | tf_op jit(solution)/shard_map/patch/pallas_call | solution.py:325
  75.9 8.1 %project_qkv.1.q_ref.k_ref.v_ref.refs_2_.refs_3_.refs_4_.refs_5_ = bf16[1024,2304]{1,0:T(8,128)(2,1)S(1)} custom-call(s32[2]{0:T(128)S(1)} %pad_add_fusion.ids_ref, bf16[1024,768]{1,0:T(8,128)(2,1)S(1)} %get-tuple-element.104.normed_ref.left_ref.refs_2_, bf16[4,48,2304]{2,1,0:T(8,128)(2,1)S(1)} %pad_maximum_fusion.2.refs_0_.refs_10_, ...), custom_call_target="tpu_custom_call" | custom-call | tf_op jit(solution)/shard_map/project_qkv/pallas_call | solution.py:362
  84.0 11.6 %attend.2 = (bf16[1024,384]{1,0:T(8,128)(2,1)S(1)}, f32[1024,128]{1,0:T(8,128)S(1)}) custom-call(s32[2]{0:T(128)S(1)} %pad_add_fusion.ids_ref, s32[1024,1]{1,0:T(8,128)S(1)} %copy.66.seg_ref.refs_1_.refs_2_, bf16[1024,2304]{1,0:T(8,128)(2,1)S(1)} %project_qkv.1.q_ref.k_ref.v_ref.refs_2_.refs_3_.refs_4_.refs_5_, ...), custom_call_target="tpu_custom_call" | custom-call | tf_op jit(solution)/shard_map/attend/pallas_call | solution.py:435
  101.2 11.6 %attend.3 = (bf16[1024,384]{1,0:T(8,128)(2,1)S(1)}, f32[1024,128]{1,0:T(8,128)S(1)}) custom-call(s32[2]{0:T(128)S(1)} %pad_add_fusion.ids_ref, bf16[4,48,3840]{2,1,0:T(8,128)(2,1)S(1)} %pad_maximum_fusion.refs_0_.refs_6_, s32[1024,1]{1,0:T(8,128)S(1)} %copy.66.seg_ref.refs_1_.refs_2_, ...), custom_call_target="tpu_custom_call" | custom-call | tf_op jit(solution)/shard_map/attend/pallas_call | solution.py:435
  114.8 15.0 %collective-permute-done.17 = bf16[2,192,768]{2,1,0:T(8,128)(2,1)S(1)} collective-permute-done((bf16[2,192,768]{2,1,0:T(8,128)(2,1)S(1)}, bf16[2,192,768]{2,1,0:T(8,128)(2,1)S(1)}, u32[]{:S(2)}, u32[]{:S(2)}) %collective-permute-start.17) | collective-permute-done | bytes 589856 | tf_op jit(solution)/shard_map/ppermute | solution.py:1015
  135.4 14.0 %feed_up.1 = (f32[1024,768]{1,0:T(8,128)S(1)}, bf16[1024,768]{1,0:T(8,128)(2,1)S(1)}, bf16[1024,3072]{1,0:T(8,128)(2,1)S(1)}, bf16[1024,3072]{1,0:T(8,128)(2,1)S(1)}) custom-call(s32[2]{0:T(128)S(1)} %pad_add_fusion.ids_ref, bf16[1024,768]{1,0:T(8,128)(2,1)S(1)} %constant_dynamic-update-slice_fusion.mixed_ref.refs_5_.refs_0_.refs_6_, ...), custom_call_target="tpu_custom_call" | custom-call | tf_op jit(solution)/shard_map/feed_up/pallas_call | solution.py:577
  151.1 9.0 %collective-permute-done.20.refs_2_ = bf16[4,192,768]{2,1,0:T(8,128)(2,1)S(1)} collective-permute-done((bf16[4,192,768]{2,1,0:T(8,128)(2,1)S(1)}, bf16[4,192,768]{2,1,0:T(8,128)(2,1)S(1)}, u32[]{:S(2)}, u32[]{:S(2)}) %collective-permute-start.20) | collective-permute-done | bytes 1179680 | tf_op jit(solution)/shard_map/ppermute | solution.py:1015
  164.9 12.8 %feed_down.1 = (bf16[1024,768]{1,0:T(8,128)(2,1)}, bf16[1024,768]{1,0:T(8,128)(2,1)S(1)}, bf16[1024,3072]{1,0:T(8,128)(2,1)S(1)}, f32[8,3072]{1,0:T(8,128)S(1)}) custom-call(s32[2]{0:T(128)S(1)} %pad_add_fusion.ids_ref, bf16[1024,3072]{1,0:T(8,128)(2,1)S(1)} %get-tuple-element.123.hidden_ref.left_ref, bf16[1024,3072]{1,0:T(8,128)(2,1)S(1)} %get-tuple-element.124.slope_ref, ...), custom_call_target="tpu_custom_call" | custom-call | tf_op jit(solution)/shard_map/feed_down/pallas_call | solution.py:650
  178.3 8.8 %grad_fc2.1 = (bf16[8,192,768]{2,1,0:T(8,128)(2,1)S(1)}, bf16[8,192,768]{2,1,0:T(8,128)(2,1)}) custom-call(s32[2]{0:T(128)S(1)} %pad_add_fusion.ids_ref, bf16[1024,3072]{1,0:T(8,128)(2,1)S(1)} %get-tuple-element.123.hidden_ref.left_ref, bf16[1024,768]{1,0:T(8,128)(2,1)S(1)} %get-tuple-element.130.right_ref.refs_4_), custom_call_target="tpu_custom_call" | custom-call | tf_op jit(solution)/shard_map/grad_fc2/pallas_call | solution.py:838
  187.2 8.9 %grad_fc1.1 = (bf16[8,48,3072]{2,1,0:T(8,128)(2,1)S(1)}, bf16[8,48,3072]{2,1,0:T(8,128)(2,1)}) custom-call(s32[2]{0:T(128)S(1)} %pad_add_fusion.ids_ref, bf16[8,192,768]{2,1,0:T(8,128)(2,1)S(1)} %get-tuple-element.131.refs_0_, bf16[8,192,768]{2,1,0:T(8,128)(2,1)} %get-tuple-element.132.refs_1_, bf16[1024,768]{1,0:T(8,128)(2,1)S(1)} %get-tuple-element.133.refs_2_, ...), custom_call_target="tpu_custom_call" | custom-call | tf_op jit(solution)/shard_map/grad_fc1/pallas_call | solution.py:838
  199.4 4.5 %add_convert_fusion.1 = (bf16[4,192,768]{2,1,0:T(8,128)(2,1)}, bf16[4,192,768]{2,1,0:T(8,128)(2,1)}) fusion(bf16[8,192,768]{2,1,0:T(8,128)(2,1)} %collective-permute-done.23, bf16[8,192,768]{2,1,0:T(8,128)(2,1)} %copy-done.24), kind=kLoop, calls=%fused_computation.7 | loop fusion | flops 4718592 | bytes 7077888 | tf_op jit(solution)/shard_map/convert_element_type | solution.py:1019
  214.2 12.4 %middle_back.1 = (f32[1024,768]{1,0:T(8,128)S(1)}, bf16[1024,768]{1,0:T(8,128)(2,1)S(1)}, bf16[1024,768]{1,0:T(8,128)(2,1)S(1)}, f32[8,768]{1,0:T(8,128)S(1)}) custom-call(s32[2]{0:T(128)S(1)} %pad_add_fusion.ids_ref, bf16[4,192,768]{2,1,0:T(8,128)(2,1)} %get-tuple-element.210.refs_0_, bf16[8,48,3072]{2,1,0:T(8,128)(2,1)S(1)} %copy-done.23, ...), custom_call_target="tpu_custom_call" | custom-call | tf_op jit(solution)/shard_map/middle_back/pallas_call | solution.py:713
  226.7 5.6 %add_convert_fusion = (bf16[8,48,1536]{2,1,0:T(8,128)(2,1)}, bf16[8,48,1536]{2,1,0:T(8,128)(2,1)}) fusion(bf16[8,48,3072]{2,1,0:T(8,128)(2,1)} %collective-permute-done.22, s32[]{:T(128)S(6)} %select_n.66, bf16[8,48,3072]{2,1,0:T(8,128)(2,1)S(1)} %copy-done.23, s32[]{:T(128)S(6)} %select_n.63), kind=kLoop, calls=%fused_computation.6 | loop fusion | flops 4718592 | bytes 7077896 | tf_op jit(solution)/shard_map/convert_element_type | solution.py:1019
  233.8 11.7 %attend_back.3.right_ref.refs_7_ = bf16[3,1024,256]{2,1,0:T(8,128)(2,1)S(1)} custom-call(s32[2]{0:T(128)S(1)} %pad_add_fusion.ids_ref, bf16[8,48,1536]{2,1,0:T(8,128)(2,1)} %get-tuple-element.208.refs_0_, s32[1024,1]{1,0:T(8,128)S(1)} %copy-done.7, bf16[1024,2304]{1,0:T(8,128)(2,1)S(1)} %bitcast.79, bf16[1024,2304]{1,0:T(8,128)(2,1)S(1)} %bitcast.79, ...), custom_call_target="tpu_custom_call" | custom-call | tf_op jit(solution)/shard_map/attend_back/pallas_call | solution.py:521
  245.6 6.7 %grad_qkv.3 = (bf16[8,48,1536]{2,1,0:T(8,128)(2,1)S(1)}, bf16[8,48,1536]{2,1,0:T(8,128)(2,1)}) custom-call(s32[2]{0:T(128)S(1)} %pad_add_fusion.ids_ref, bf16[1024,768]{1,0:T(8,128)(2,1)S(1)} %get-tuple-element.104.normed_ref.left_ref.refs_2_, bf16[3,1024,256]{2,1,0:T(8,128)(2,1)S(1)} %attend_back.3.right_ref.refs_7_, ...), custom_call_target="tpu_custom_call" | custom-call | tf_op jit(solution)/shard_map/grad_qkv/pallas_call | solution.py:838
  259.3 11.8 %attend_back.4.refs_3_.refs_8_ = bf16[3,1024,256]{2,1,0:T(8,128)(2,1)S(1)} custom-call(s32[2]{0:T(128)S(1)} %pad_add_fusion.ids_ref, bf16[2,192,768]{2,1,0:T(8,128)(2,1)S(1)} %get-tuple-element.214.refs_0_, bf16[8,48,1536]{2,1,0:T(8,128)(2,1)S(1)} %copy-done.40, s32[1024,1]{1,0:T(8,128)S(1)} %copy-done.8, bf16[1024,2304]{1,0:T(8,128)(2,1)S(1)} %copy-done.1, ...), custom_call_target="tpu_custom_call" | custom-call | tf_op jit(solution)/shard_map/attend_back/pallas_call | solution.py:521
  280.6 6.3 %collective-permute-done.27 = bf16[2,192,768]{2,1,0:T(8,128)(2,1)S(1)} collective-permute-done((bf16[2,192,768]{2,1,0:T(8,128)(2,1)S(1)}, bf16[2,192,768]{2,1,0:T(8,128)(2,1)S(1)}, u32[]{:S(2)}, u32[]{:S(2)}) %collective-permute-start.27) | collective-permute-done | bytes 589856 | tf_op jit(solution)/shard_map/ppermute | solution.py:1015
  286.9 12.0 %attend_back.5.refs_3_.refs_9_ = bf16[3,1024,256]{2,1,0:T(8,128)(2,1)S(1)} custom-call(s32[2]{0:T(128)S(1)} %pad_add_fusion.ids_ref, bf16[1,192,768]{2,1,0:T(8,128)(2,1)S(1)} %add_convert_fusion.24.refs_0_, bf16[8,48,768]{2,1,0:T(8,128)(2,1)S(1)} %get-tuple-element.149.refs_1_, s32[1024,1]{1,0:T(8,128)S(1)} %copy-done.8, bf16[1024,2304]{1,0:T(8,128)(2,1)S(1)} %bitcast.81, ...), custom_call_target="tpu_custom_call" | custom-call | tf_op jit(solution)/shard_map/attend_back/pallas_call | solution.py:521
  309.8 10.1 %embed_back.1 = (bf16[1024,768]{1,0:T(8,128)(2,1)S(1)}, bf16[16,1024]{1,0:T(8,128)(2,1)S(1)}) custom-call(s32[2]{0:T(128)S(1)} %pad_add_fusion.ids_ref, bf16[8,48,768]{2,1,0:T(8,128)(2,1)S(1)} %get-tuple-element.154.refs_0_, bf16[2,48,1536]{2,1,0:T(8,128)(2,1)S(1)} %get-tuple-element.220.refs_1_, f32[1024,768]{1,0:T(8,128)S(1)} %copy-done.18, ...), custom_call_target="tpu_custom_call" | custom-call | tf_op jit(solution)/shard_map/embed_back/pallas_call | solution.py:911
  345.9 4.8 %collective-permute-done.37 = bf16[208,1024]{1,0:T(8,128)(2,1)S(1)} collective-permute-done((bf16[208,1024]{1,0:T(8,128)(2,1)S(1)}, bf16[208,1024]{1,0:T(8,128)(2,1)S(1)}, u32[]{:S(2)}, u32[]{:S(2)}) %collective-permute-start.37) | collective-permute-done | bytes 426016 | tf_op jit(solution)/shard_map/ppermute | solution.py:1015
  400.3 4.1 collective-permute-start.57
  (426 shorter events, 192.3 us)
Async XLA Ops:
  50.6 22.4 %collective-permute-start.10 = (bf16[4,48,2304]{2,1,0:T(8,128)(2,1)S(1)}, bf16[4,48,2304]{2,1,0:T(8,128)(2,1)}, u32[]{:S(2)}, u32[]{:S(2)}) collective-permute-start(bf16[4,48,2304]{2,1,0:T(8,128)(2,1)S(1)} %pad_maximum_fusion.2.refs_0_.refs_10_), channel_id=1, source_target_pairs={{0,4},{2,6},{4,0},{6,2},{8,12},{10,14},{12,8},{14,10},{16,20},{18,... | collective-permute-start | bytes 2654216 | tf_op jit(solution)/shard_map/ppermute | solution.py:1015
  52.9 20.1 %collective-permute-start.12 = (bf16[1,48,3840]{2,1,0:T(8,128)(2,1)}, bf16[1,48,3840]{2,1,0:T(8,128)(2,1)}, u32[]{:S(2)}, u32[]{:S(2)}) collective-permute-start(bf16[1,48,3840]{2,1,0:T(8,128)(2,1)} %pad_maximum_fusion.8), channel_id=1, source_target_pairs={{0,16},{2,18},{4,20},{6,22},{8,24},{10,26},{12,28},{14,30},{16,0},... | collective-permute-start | bytes 1105928 | tf_op jit(solution)/shard_map/ppermute | solution.py:1015
  58.0 17.8 %collective-permute-start.9 = (bf16[4,48,2304]{2,1,0:T(8,128)(2,1)S(1)}, bf16[4,48,2304]{2,1,0:T(8,128)(2,1)}, u32[]{:S(2)}, u32[]{:S(2)}) collective-permute-start(bf16[4,48,2304]{2,1,0:T(8,128)(2,1)S(1)} %pad_maximum_fusion.2.refs_0_.refs_10_), channel_id=1, source_target_pairs={{0,2},{2,0},{4,6},{6,4},{8,10},{10,8},{12,14},{14,12},{16,18},{18,... | collective-permute-start | bytes 2654216 | tf_op jit(solution)/shard_map/ppermute | solution.py:1015
  74.9 20.6 %collective-permute-start.13 = (bf16[2,48,3840]{2,1,0:T(8,128)(2,1)}, bf16[2,48,3840]{2,1,0:T(8,128)(2,1)}, u32[]{:S(2)}, u32[]{:S(2)}) collective-permute-start(bf16[2,48,3840]{2,1,0:T(8,128)(2,1)} %pad_maximum_fusion.3), channel_id=1, source_target_pairs={{0,8},{2,10},{4,12},{6,14},{8,0},{10,2},{12,4},{14,6},{16,24},{18,... | collective-permute-start | bytes 2211848 | tf_op jit(solution)/shard_map/ppermute | solution.py:1015
  97.1 34.4 %collective-permute-start.15 = (bf16[4,48,3840]{2,1,0:T(8,128)(2,1)S(1)}, bf16[4,48,3840]{2,1,0:T(8,128)(2,1)S(1)}, u32[]{:S(2)}, u32[]{:S(2)}) collective-permute-start(bf16[4,48,3840]{2,1,0:T(8,128)(2,1)S(1)} %pad_maximum_fusion.refs_0_.refs_6_), channel_id=1, source_target_pairs={{0,4},{2,6},{4,0},{6,2},{8,12},{10,14},{12,8},{14,10},{16,20},{18,... | collective-permute-start | bytes 4423688 | tf_op jit(solution)/shard_map/ppermute | solution.py:1015
  98.4 16.2 %collective-permute-start.16 = (bf16[1,192,768]{2,1,0:T(8,128)(2,1)S(1)}, bf16[1,192,768]{2,1,0:T(8,128)(2,1)S(1)}, u32[]{:S(2)}, u32[]{:S(2)}) collective-permute-start(bf16[1,192,768]{2,1,0:T(8,128)(2,1)S(1)} %convert_bitcast_fusion), channel_id=1, source_target_pairs={{0,16},{2,18},{4,20},{6,22},{8,24},{10,26},{12,28},{14,30},{16,0},... | collective-permute-start | bytes 884744 | tf_op jit(solution)/shard_map/ppermute | solution.py:1015
  114.6 15.2 %collective-permute-start.17 = (bf16[2,192,768]{2,1,0:T(8,128)(2,1)S(1)}, bf16[2,192,768]{2,1,0:T(8,128)(2,1)S(1)}, u32[]{:S(2)}, u32[]{:S(2)}) collective-permute-start(bf16[2,192,768]{2,1,0:T(8,128)(2,1)S(1)} %pad_maximum_fusion.5), channel_id=1, source_target_pairs={{0,8},{2,10},{4,12},{6,14},{8,0},{10,2},{12,4},{14,6},{16,24},{18,... | collective-permute-start | bytes 1769480 | tf_op jit(solution)/shard_map/ppermute | solution.py:1015
  114.7 18.8 %collective-permute-start.14 = (bf16[4,48,3840]{2,1,0:T(8,128)(2,1)S(1)}, bf16[4,48,3840]{2,1,0:T(8,128)(2,1)S(1)}, u32[]{:S(2)}, u32[]{:S(2)}) collective-permute-start(bf16[4,48,3840]{2,1,0:T(8,128)(2,1)S(1)} %pad_maximum_fusion.refs_0_.refs_6_), channel_id=1, source_target_pairs={{0,2},{2,0},{4,6},{6,4},{8,10},{10,8},{12,14},{14,12},{16,18},{18,... | collective-permute-start | bytes 4423688 | tf_op jit(solution)/shard_map/ppermute | solution.py:1015
  131.7 28.4 %collective-permute-start.20 = (bf16[4,192,768]{2,1,0:T(8,128)(2,1)S(1)}, bf16[4,192,768]{2,1,0:T(8,128)(2,1)S(1)}, u32[]{:S(2)}, u32[]{:S(2)}) collective-permute-start(bf16[4,192,768]{2,1,0:T(8,128)(2,1)S(1)} %pad_maximum_fusion.1.refs_0_), channel_id=1, source_target_pairs={{0,4},{2,6},{4,0},{6,2},{8,12},{10,14},{12,8},{14,10},{16,20},{18,... | collective-permute-start | bytes 3538952 | tf_op jit(solution)/shard_map/ppermute | solution.py:1015
  133.2 26.9 %collective-permute-start.19 = (bf16[4,192,768]{2,1,0:T(8,128)(2,1)S(1)}, bf16[4,192,768]{2,1,0:T(8,128)(2,1)S(1)}, u32[]{:S(2)}, u32[]{:S(2)}) collective-permute-start(bf16[4,192,768]{2,1,0:T(8,128)(2,1)S(1)} %pad_maximum_fusion.1.refs_0_), channel_id=1, source_target_pairs={{0,2},{2,0},{4,6},{6,4},{8,10},{10,8},{12,14},{14,12},{16,18},{18,... | collective-permute-start | bytes 3538952 | tf_op jit(solution)/shard_map/ppermute | solution.py:1015
  197.6 29.0 %collective-permute-start.22 = (bf16[8,48,3072]{2,1,0:T(8,128)(2,1)}, bf16[8,48,3072]{2,1,0:T(8,128)(2,1)}, u32[]{:S(2)}, u32[]{:S(2)}) collective-permute-start(bf16[8,48,3072]{2,1,0:T(8,128)(2,1)} %get-tuple-element.136), channel_id=1, source_target_pairs={{0,2},{2,0},{4,6},{6,4},{8,10},{10,8},{12,14},{14,12},{16,18},{18,... | collective-permute-start | bytes 7077896 | tf_op jit(solution)/shard_map/ppermute | solution.py:1015
  203.9 49.3 %collective-permute-start.25 = (bf16[4,192,768]{2,1,0:T(8,128)(2,1)}, bf16[4,192,768]{2,1,0:T(8,128)(2,1)}, u32[]{:S(2)}, u32[]{:S(2)}) collective-permute-start(bf16[4,192,768]{2,1,0:T(8,128)(2,1)} %get-tuple-element.210.refs_0_), channel_id=1, source_target_pairs={{0,4},{2,6},{4,0},{6,2},{8,12},{10,14},{12,8},{14,10},{16,20},{18,... | collective-permute-start | bytes 3538952 | tf_op jit(solution)/shard_map/ppermute | solution.py:1015
  232.3 40.1 %collective-permute-start.28 = (bf16[8,48,1536]{2,1,0:T(8,128)(2,1)}, bf16[8,48,1536]{2,1,0:T(8,128)(2,1)}, u32[]{:S(2)}, u32[]{:S(2)}) collective-permute-start(bf16[8,48,1536]{2,1,0:T(8,128)(2,1)} %get-tuple-element.208.refs_0_), channel_id=1, source_target_pairs={{0,1},{1,0},{2,3},{3,2},{4,5},{5,4},{6,7},{7,6},{8,9},{9,8},{10,11... | collective-permute-start | bytes 3538952 | tf_op jit(solution)/shard_map/ppermute | solution.py:1015
  253.3 19.1 %collective-permute-start.24 = (bf16[8,48,1536]{2,1,0:T(8,128)(2,1)}, bf16[8,48,1536]{2,1,0:T(8,128)(2,1)}, u32[]{:S(2)}, u32[]{:S(2)}) collective-permute-start(bf16[8,48,1536]{2,1,0:T(8,128)(2,1)} %get-tuple-element.145), channel_id=1, source_target_pairs={{0,2},{2,0},{4,6},{6,4},{8,10},{10,8},{12,14},{14,12},{16,18},{18,... | collective-permute-start | bytes 3538952 | tf_op jit(solution)/shard_map/ppermute | solution.py:1015
  271.0 15.8 %collective-permute-start.27 = (bf16[2,192,768]{2,1,0:T(8,128)(2,1)S(1)}, bf16[2,192,768]{2,1,0:T(8,128)(2,1)S(1)}, u32[]{:S(2)}, u32[]{:S(2)}) collective-permute-start(bf16[2,192,768]{2,1,0:T(8,128)(2,1)S(1)} %get-tuple-element.214.refs_0_), channel_id=1, source_target_pairs={{0,8},{2,10},{4,12},{6,14},{8,0},{10,2},{12,4},{14,6},{16,24},{18,... | collective-permute-start | bytes 1769480 | tf_op jit(solution)/shard_map/ppermute | solution.py:1015
  274.1 24.8 %collective-permute-start.26 = (bf16[8,48,768]{2,1,0:T(8,128)(2,1)S(1)}, bf16[8,48,768]{2,1,0:T(8,128)(2,1)S(1)}, u32[]{:S(2)}, u32[]{:S(2)}) collective-permute-start(bf16[8,48,768]{2,1,0:T(8,128)(2,1)S(1)} %get-tuple-element.215.refs_0_), channel_id=1, source_target_pairs={{0,1},{1,0},{2,3},{3,2},{4,5},{5,4},{6,7},{7,6},{8,9},{9,8},{10,11... | collective-permute-start | bytes 1769480 | tf_op jit(solution)/shard_map/ppermute | solution.py:1015
  279.4 22.8 %collective-permute-start.29 = (bf16[8,48,768]{2,1,0:T(8,128)(2,1)S(1)}, bf16[8,48,768]{2,1,0:T(8,128)(2,1)S(1)}, u32[]{:S(2)}, u32[]{:S(2)}) collective-permute-start(bf16[8,48,768]{2,1,0:T(8,128)(2,1)S(1)} %get-tuple-element.152), channel_id=1, source_target_pairs={{0,2},{2,0},{4,6},{6,4},{8,10},{10,8},{12,14},{14,12},{16,18},{18,... | collective-permute-start | bytes 1769480 | tf_op jit(solution)/shard_map/ppermute | solution.py:1015
  279.5 26.9 %collective-permute-start.31 = (bf16[4,48,1536]{2,1,0:T(8,128)(2,1)S(1)}, bf16[4,48,1536]{2,1,0:T(8,128)(2,1)S(1)}, u32[]{:S(2)}, u32[]{:S(2)}) collective-permute-start(bf16[4,48,1536]{2,1,0:T(8,128)(2,1)S(1)} %get-tuple-element.212.refs_1_), channel_id=1, source_target_pairs={{0,4},{2,6},{4,0},{6,2},{8,12},{10,14},{12,8},{14,10},{16,20},{18,... | collective-permute-start | bytes 1769480 | tf_op jit(solution)/shard_map/ppermute | solution.py:1015
  298.9 21.1 %collective-permute-start.33 = (bf16[1,192,768]{2,1,0:T(8,128)(2,1)S(1)}, bf16[1,192,768]{2,1,0:T(8,128)(2,1)S(1)}, u32[]{:S(2)}, u32[]{:S(2)}) collective-permute-start(bf16[1,192,768]{2,1,0:T(8,128)(2,1)S(1)} %add_convert_fusion.24.refs_0_), channel_id=1, source_target_pairs={{0,16},{2,18},{4,20},{6,22},{8,24},{10,26},{12,28},{14,30},{16,0},... | collective-permute-start | bytes 884744 | tf_op jit(solution)/shard_map/ppermute | solution.py:1015
  308.3 22.1 %collective-permute-start.35 = (bf16[4,48,768]{2,1,0:T(8,128)(2,1)S(1)}, bf16[4,48,768]{2,1,0:T(8,128)(2,1)}, u32[]{:S(2)}, u32[]{:S(2)}) collective-permute-start(bf16[4,48,768]{2,1,0:T(8,128)(2,1)S(1)} %get-tuple-element.167.refs_1_), channel_id=1, source_target_pairs={{0,4},{2,6},{4,0},{6,2},{8,12},{10,14},{12,8},{14,10},{16,20},{18,... | collective-permute-start | bytes 884744 | tf_op jit(solution)/shard_map/ppermute | solution.py:1015
  309.3 20.0 %collective-permute-start.36 = (bf16[2,48,1536]{2,1,0:T(8,128)(2,1)S(1)}, bf16[2,48,1536]{2,1,0:T(8,128)(2,1)}, u32[]{:S(2)}, u32[]{:S(2)}) collective-permute-start(bf16[2,48,1536]{2,1,0:T(8,128)(2,1)S(1)} %get-tuple-element.220.refs_1_), channel_id=1, source_target_pairs={{0,8},{2,10},{4,12},{6,14},{8,0},{10,2},{12,4},{14,6},{16,24},{18,... | collective-permute-start | bytes 884744 | tf_op jit(solution)/shard_map/ppermute | solution.py:1015
  332.6 18.3 %collective-permute-start.42 = (bf16[1,48,1536]{2,1,0:T(8,128)(2,1)S(1)}, bf16[1,48,1536]{2,1,0:T(8,128)(2,1)S(1)}, u32[]{:S(2)}, u32[]{:S(2)}) collective-permute-start(bf16[1,48,1536]{2,1,0:T(8,128)(2,1)S(1)} %add_convert_fusion.33), channel_id=1, source_target_pairs={{0,16},{2,18},{4,20},{6,22},{8,24},{10,26},{12,28},{14,30},{16,0},... | collective-permute-start | bytes 442376 | tf_op jit(solution)/shard_map/ppermute | solution.py:1015
  332.7 19.2 %collective-permute-start.41 = (bf16[2,48,768]{2,1,0:T(8,128)(2,1)S(1)}, bf16[2,48,768]{2,1,0:T(8,128)(2,1)S(1)}, u32[]{:S(2)}, u32[]{:S(2)}) collective-permute-start(bf16[2,48,768]{2,1,0:T(8,128)(2,1)S(1)} %get-tuple-element.230), channel_id=1, source_target_pairs={{0,8},{2,10},{4,12},{6,14},{8,0},{10,2},{12,4},{14,6},{16,24},{18,... | collective-permute-start | bytes 442376 | tf_op jit(solution)/shard_map/ppermute | solution.py:1015
  382.6 30.9 %all-to-all-start = ((bf16[16,48,192]{2,1,0:T(8,128)(2,1)}), bf16[16,48,192]{2,1,0:T(8,128)(2,1)S(1)}, u32[]{:S(2)}, u32[]{:S(2)}) async-start(bf16[16,48,192]{2,1,0:T(8,128)(2,1)} %bitcast.77), calls=%async_computation | async-start | bytes 786432 | tf_op jit(solution)/shard_map/all_to_all | solution.py:1434
  (136 other events, 1246.5 us)
